TPU v7x, 32 devices: a whole 2x2x4 slice. The times are simulated.
32 devices in a mesh: section: 2 (over core), dp: 4 (over z), mp: 4 (over y, x).
Axes of the slice: x: 2, y: 2, z: 4, core: 2. Of those that a mesh axis runs over, the one named last changes fastest.
Arguments:
- features: bfloat16 [4096, 4096], P(('section', 'dp'), 'mp'), may hold values from -6 to 6
- w_in: bfloat16 [4096, 2048], P(('section', 'dp'), 'mp'), may hold values from -0.09375 to 0.09375
- w_out: bfloat16 [512, 2048], P(('section', 'dp'), 'mp'), may hold values from -0.125 to 0.125
- codebook: bfloat16 [3, 65536, 512], P(None, ('section', 'dp'), 'mp'), may hold values from -3 to 3
- codes: int32 [3, 4096], P(None, ('section', 'dp')), may hold values from 0 to 65535, as said below
- decoder_grad: bfloat16 [4096, 512], P(('section', 'dp'), 'mp'), may hold values from -6 to 6
Outputs:
- in_grad: float32 [4096, 2048], P(('section', 'dp'), 'mp')
- out_grad: float32 [512, 2048], P(('section', 'dp'), 'mp')
- code_sums: float32 [3, 65536, 512], P(None, ('section', 'dp'), 'mp')
Inputs may be any that keep to these rules, and one draw needn't show every extreme that they name: Row k of a level's codebook belongs to owner k // 8192. Within the 512 items of one device (aligned blocks of items), at each level at most 128 codes belong to one owner; at each level some owner receives exactly 128 codes from every device's items.
All inputs are finite; a program needn't handle non-finite values.
Results may differ from a plain program's by a relative error of at most 0.0026.
Values may be sent and summed in bfloat16 or wider, within the bound.
A program may use at most 64 MiB of HBM per device.

v0:
```python
import jax
import jax.numpy as jnp
from jax import lax
from jax.sharding import PartitionSpec as P

BETA = 0.25


def silu_slope(preact):
    logistic = jax.nn.sigmoid(preact)
    return logistic * (1.0 + preact * (1.0 - logistic))


def send_requests(outgoing):
    return lax.all_to_all(outgoing, ("section", "dp"), split_axis=0, concat_axis=0, tiled=True)


def send_rows(outgoing):
    return lax.all_to_all(outgoing, ("section", "dp"), split_axis=0, concat_axis=0, tiled=True)


def send_sums(outgoing):
    return lax.all_to_all(outgoing, ("section", "dp"), split_axis=0, concat_axis=0, tiled=True)


def shards(features, w_in, w_out, codebook, codes, decoder_grad):
    owners = lax.axis_size(("section", "dp"))
    item_rows = features.shape[0]
    levels, rows_own, width_part = codebook.shape
    capacity = max(2, 2 * item_rows // owners)
    items_all = item_rows * owners
    all_features = lax.all_gather(features, "mp", axis=1, tiled=True)
    half_rows = lax.all_gather(w_in, "dp", axis=0, tiled=True)
    preact = jnp.dot(
        all_features,
        lax.all_gather(half_rows, "section", axis=0, tiled=True),
        preferred_element_type=jnp.float32,
    )
    hidden = jax.nn.silu(preact).astype(jnp.bfloat16)
    out_full = lax.all_gather(w_out, ("section", "dp"), axis=0, tiled=True)
    latent_part = lax.dot_general(
        hidden, out_full, (((1,), (1,)), ((), ())), preferred_element_type=jnp.float32
    )
    latent = lax.psum_scatter(latent_part, "mp", scatter_dimension=1, tiled=True)
    owner_of = codes // rows_own
    level_ids = jnp.arange(levels, dtype=jnp.int32)[:, None]
    flat_rows = codes % rows_own + level_ids * rows_own
    matches = (owner_of[:, :, None] == jnp.arange(owners, dtype=jnp.int32)).astype(jnp.int32)
    ranking = jnp.sum(jnp.cumsum(matches, axis=1) * matches, axis=2) - 1
    flat_book = codebook.reshape(levels * rows_own, width_part)
    slot_of = owner_of * capacity + ranking
    requests = (
        jnp.zeros((levels, owners * capacity), jnp.int32).at[level_ids, slot_of].set(flat_rows)
    )
    asked_list = []
    fetched_list = []
    for level_index in range(levels):
        asked_rows = send_requests(requests[level_index].reshape(owners, capacity))
        rows_back = send_rows(jnp.take(flat_book, asked_rows, axis=0))
        asked_list.append(asked_rows)
        fetched_list.append(
            jnp.take(rows_back.reshape(owners * capacity, width_part), slot_of[level_index], axis=0)
        )
    codewords = jnp.stack(fetched_list)
    residual = latent
    pull_sum = jnp.zeros_like(latent)
    inputs = []
    for level_index in range(levels):
        inputs.append(residual)
        residual = residual - codewords[level_index].astype(jnp.float32)
        pull_sum = pull_sum + residual
    code_total = jnp.zeros((levels * rows_own, width_part), jnp.float32)
    for level_index in range(levels):
        outgoing = (
            jnp.zeros((owners * capacity, width_part), jnp.float32)
            .at[slot_of[level_index]]
            .set(inputs[level_index])
        )
        incoming = send_sums(outgoing.reshape(owners, capacity, width_part))
        code_total = code_total.at[asked_list[level_index].reshape(-1)].add(
            incoming.reshape(-1, width_part)
        )
    code_sums = code_total.reshape(levels, rows_own, width_part)
    latent_grad = (
        (decoder_grad.astype(jnp.float32) + 2.0 * BETA * pull_sum)
        / jnp.sqrt(jnp.float32(items_all))
    ).astype(jnp.bfloat16)
    grad_full = lax.all_gather(latent_grad, "mp", axis=1, tiled=True)
    out_grad = lax.psum_scatter(
        lax.dot_general(
            grad_full, hidden, (((0,), (0,)), ((), ())), preferred_element_type=jnp.float32
        ),
        ("section", "dp"),
        scatter_dimension=0,
        tiled=True,
    )
    back_hidden = jnp.dot(grad_full, out_full, preferred_element_type=jnp.float32)
    pre_grad = (back_hidden * silu_slope(preact)).astype(jnp.bfloat16)
    half_grad = lax.psum_scatter(
        lax.dot_general(
            all_features, pre_grad, (((0,), (0,)), ((), ())), preferred_element_type=jnp.float32
        ),
        "section",
        scatter_dimension=0,
        tiled=True,
    )
    in_grad = lax.psum_scatter(half_grad, "dp", scatter_dimension=0, tiled=True)
    return (in_grad, out_grad, code_sums)


def solution(mesh):
    in_specs = (
        P(("section", "dp"), "mp"),
        P(("section", "dp"), "mp"),
        P(("section", "dp"), "mp"),
        P(None, ("section", "dp"), "mp"),
        P(None, ("section", "dp")),
        P(("section", "dp"), "mp"),
    )
    out_specs = (
        P(("section", "dp"), "mp"),
        P(("section", "dp"), "mp"),
        P(None, ("section", "dp"), "mp"),
    )
    return jax.shard_map(shards, mesh=mesh, in_specs=in_specs, out_specs=out_specs, check_vma=False)
```

profile of v0, /device:TPU:8, one launch (start us, length us, event | category | flops | bytes accessed | tf_op | source)
XLA Modules:
  0.0 376.4 jit_solution(4008309919525406187)
XLA Ops:
  7.2 0.7 all-gather.6.cloned.1.call-update
  7.9 0.7 all-gather.4.cloned.1.call-update
  8.7 46.4 %all-gather.6.cloned.1.call-done = bf16[2048,512]{1,0:T(8,128)(2,1)} async-done(((bf16[512,512]{1,0:T(8,128)(2,1)}), bf16[2048,512]{1,0:T(8,128)(2,1)}) %all-gather.6.cloned.1.call-update) | async-done | bytes 2097168 | tf_op jit(solution)/shard_map/all_gather | solution.py:33
  55.1 0.8 fusion.16
  55.9 3.4 reduce-window.6
  59.9 0.7 multiply_reduce_fusion
  60.6 0.7 and_reduce_fusion
  61.4 6.2 %scatter_custom_fusion.6 = s32[3072]{0:T(1024)S(1)} fusion(s32[1536]{0:T(1024)S(1)} %reshape.377, s32[1536]{0:T(1024)S(1)} %reshape.379, s32[]{:T(128)} %constant.45.clone.1), kind=kCustom, calls=%fused_computation.67 | custom fusion | bytes 12292
  67.6 0.6 fusion.22
  68.2 5.4 %all-to-all-start.4 = ((s32[8,1,128]{2,1,0:T(1,128)}), s32[8,1,128]{2,1,0:T(1,128)S(1)}, u32[]{:S(2)}, u32[]{:S(2)}) async-start(s32[8,1,128]{2,1,0:T(1,128)} %bitcast.17), calls=%async_computation.5 | async-start | bytes 8192 | tf_op jit(solution)/shard_map/all_to_all | solution.py:15
  73.6 27.1 %all_gather.18 = bf16[512,512]{1,0:T(8,128)(2,1)S(1)} all-gather(bf16[64,512]{1,0:T(8,128)(2,1)} %param.12), channel_id=1, replica_groups=mesh['section'=2,'dp'=4,'mp'=4] {'section','dp'}, dimensions={0}, use_global_device_ids=true | all-gather | bytes 589824 | tf_op jit(solution)/shard_map/all_gather | solution.py:40
  100.7 4.9 %all-to-all-start = ((s32[8,1,128]{2,1,0:T(1,128)}), s32[8,1,128]{2,1,0:T(1,128)S(1)}, u32[]{:S(2)}, u32[]{:S(2)}) async-start(s32[8,1,128]{2,1,0:T(1,128)} %bitcast.4), calls=%async_computation.1 | async-start | bytes 8192 | tf_op jit(solution)/shard_map/all_to_all | solution.py:15
  105.6 6.5 %gather_fusion.4 = bf16[1024,128]{1,0:T(8,128)(2,1)S(1)} fusion(bf16[24576,128]{1,0:T(8,128)(2,1)} %bitcast.74, s32[1024]{0:T(1024)S(1)} %bitcast_clamp_fusion), kind=kCustom, calls=%fused_computation.3.clone | custom fusion | bytes 528384 | tf_op jit(solution)/shard_map/jit(_take)/gather | solution.py:59
  112.1 13.4 %all-gather.8.cloned.1.call-done = bf16[4096,512]{1,0:T(8,128)(2,1)} async-done(((bf16[2048,512]{1,0:T(8,128)(2,1)}), bf16[4096,512]{1,0:T(8,128)(2,1)}) %all-gather.8.cloned.1.call-update) | async-done | bytes 4194320 | tf_op jit(solution)/shard_map/all_gather | solution.py:36
  125.6 5.9 %multiply_convert_fusion = (bf16[512,512]{1,0:T(8,128)(2,1)S(1)}, f32[512,512]{1,0:T(8,128)S(1)}) fusion(bf16[512,4096]{1,0:T(8,128)(2,1)} %all-gather.4.cloned.1.call-done, bf16[4096,512]{1,0:T(8,128)(2,1)} %all-gather.8.cloned.1.call-done), kind=kOutput, calls=%fused_computation.22 | convolution fusion | flops 2148794368 | bytes 9961472 | tf_op jit(solution)/shard_map/dot_general | solution.py:34
  131.5 1.4 fusion.24
  133.0 0.9 broadcast_select_fusion
  133.9 5.1 %all-to-all-start.2 = ((s32[8,1,128]{2,1,0:T(1,128)}), s32[8,1,128]{2,1,0:T(1,128)S(1)}, u32[]{:S(2)}, u32[]{:S(2)}) async-start(s32[8,1,128]{2,1,0:T(1,128)} %bitcast.11), calls=%async_computation.3 | async-start | bytes 8192 | tf_op jit(solution)/shard_map/all_to_all | solution.py:15
  139.0 6.7 %gather_fusion = bf16[1024,128]{1,0:T(8,128)(2,1)S(1)} fusion(bf16[24576,128]{1,0:T(8,128)(2,1)} %bitcast.75, s32[1024]{0:T(1024)S(1)} %bitcast_clamp_fusion.2), kind=kCustom, calls=%fused_computation.clone | custom fusion | bytes 528384 | tf_op jit(solution)/shard_map/jit(_take)/gather | solution.py:59
  145.7 5.1 %all-to-all-start.5 = ((bf16[8,128,128]{2,1,0:T(8,128)(2,1)}), bf16[8,128,128]{2,1,0:T(8,128)(2,1)S(1)}, u32[]{:S(2)}, u32[]{:S(2)}) async-start(bf16[8,128,128]{2,1,0:T(8,128)(2,1)} %broadcast_select_fusion), calls=%async_computation.6 | async-start | bytes 524288 | tf_op jit(solution)/shard_map/all_to_all | solution.py:19
  150.8 6.5 %gather_fusion.2 = bf16[1024,128]{1,0:T(8,128)(2,1)S(1)} fusion(bf16[24576,128]{1,0:T(8,128)(2,1)} %bitcast.76, s32[1024]{0:T(1024)S(1)} %bitcast_clamp_fusion.1), kind=kCustom, calls=%fused_computation.2.clone | custom fusion | bytes 528384 | tf_op jit(solution)/shard_map/jit(_take)/gather | solution.py:59
  157.3 0.9 broadcast_select_fusion.2
  158.2 5.3 %all-to-all-start.1 = ((bf16[8,128,128]{2,1,0:T(8,128)(2,1)}), bf16[8,128,128]{2,1,0:T(8,128)(2,1)S(1)}, u32[]{:S(2)}, u32[]{:S(2)}) async-start(bf16[8,128,128]{2,1,0:T(8,128)(2,1)} %broadcast_select_fusion.2), calls=%async_computation.2 | async-start | bytes 524288 | tf_op jit(solution)/shard_map/all_to_all | solution.py:19
  163.5 0.9 broadcast_select_fusion.1
  164.5 5.4 %all-to-all-done.1 = bf16[8,128,128]{2,1,0:T(8,128)(2,1)S(1)} async-done(((bf16[8,128,128]{2,1,0:T(8,128)(2,1)}), bf16[8,128,128]{2,1,0:T(8,128)(2,1)S(1)}, u32[]{:S(2)}, u32[]{:S(2)}) %all-to-all-start.1) | async-done | bytes 262176 | tf_op jit(solution)/shard_map/all_to_all | solution.py:19
  169.8 6.4 %all-to-all-start.3 = ((bf16[8,128,128]{2,1,0:T(8,128)(2,1)}), bf16[8,128,128]{2,1,0:T(8,128)(2,1)S(1)}, u32[]{:S(2)}, u32[]{:S(2)}) async-start(bf16[8,128,128]{2,1,0:T(8,128)(2,1)} %broadcast_select_fusion.1), calls=%async_computation.4 | async-start | bytes 524288 | tf_op jit(solution)/shard_map/all_to_all | solution.py:19
  176.3 1.3 gather_fusion.5
  177.6 1.3 gather_fusion.1
  179.0 3.6 all-to-all-done.3
  182.5 1.3 gather_fusion.3
  183.9 1.2 multiply_convert_fusion.1
  185.2 10.8 %all_gather.19 = bf16[512,512]{1,0:T(8,128)(2,1)S(1)} all-gather(bf16[512,128]{1,0:T(8,128)(2,1)S(1)} %multiply_convert_fusion.1), channel_id=1, replica_groups=mesh['section'=2,'dp'=4,'mp'=4] {'mp'}, dimensions={1}, use_global_device_ids=true | all-gather | bytes 655360 | tf_op jit(solution)/shard_map/all_gather | solution.py:88
  196.0 8.5 %convolution_bitcast_fusion = f32[4096,512]{0,1:T(8,128)} fusion(bf16[512,4096]{1,0:T(8,128)(2,1)} %all-gather.4.cloned.1.call-done, bf16[512,512]{1,0:T(8,128)(2,1)S(1)} %all_gather.19, bf16[512,512]{1,0:T(8,128)(2,1)S(1)} %all_gather.18, f32[512,512]{1,0:T(8,128)S(1)} %get-tuple-element.28), kind=kOutput, calls=%fused_computation.13 | convolution fusion | flops 2418278400 | bytes 14680064 | tf_op jit(solution)/shard_map/dot_general | solution.py:100
  204.6 16.6 %reduce-scatter.7.cloned.1.call-done = f32[2048,512]{0,1:T(8,128)} async-done(((f32[4096,512]{0,1:T(8,128)}), f32[2048,512]{0,1:T(8,128)}) %reduce-scatter.7.cloned.1.call-update) | async-done | bytes 4194320 | tf_op jit(solution)/shard_map/reduce_scatter | solution.py:99
  221.2 2.6 scatter_custom_fusion.2
  223.8 5.1 %all-to-all-start.7 = ((f32[8,128,128]{2,1,0:T(8,128)}), f32[8,128,128]{2,1,0:T(8,128)S(1)}, u32[]{:S(2)}, u32[]{:S(2)}) async-start(f32[8,128,128]{2,1,0:T(8,128)} %bitcast.33), calls=%async_computation.11 | async-start | bytes 1048576 | tf_op jit(solution)/shard_map/all_to_all | solution.py:23
  229.0 1.5 fusion.25
  230.4 2.5 scatter_custom_fusion
  232.9 19.1 %all-to-all-done.7 = f32[8,128,128]{2,1,0:T(8,128)S(1)} async-done(((f32[8,128,128]{2,1,0:T(8,128)}), f32[8,128,128]{2,1,0:T(8,128)S(1)}, u32[]{:S(2)}, u32[]{:S(2)}) %all-to-all-start.7) | async-done | bytes 524320 | tf_op jit(solution)/shard_map/all_to_all | solution.py:23
  252.1 8.2 %all-to-all-start.6 = ((f32[8,128,128]{2,1,0:T(8,128)}), f32[8,128,128]{2,1,0:T(8,128)S(1)}, u32[]{:S(2)}, u32[]{:S(2)}) async-start(f32[8,128,128]{2,1,0:T(8,128)} %bitcast.27), calls=%async_computation.10 | async-start | bytes 1048576 | tf_op jit(solution)/shard_map/all_to_all | solution.py:23
  260.3 2.7 scatter_custom_fusion.4
  263.0 23.4 %all-to-all-done.6 = f32[8,128,128]{2,1,0:T(8,128)S(1)} async-done(((f32[8,128,128]{2,1,0:T(8,128)}), f32[8,128,128]{2,1,0:T(8,128)S(1)}, u32[]{:S(2)}, u32[]{:S(2)}) %all-to-all-start.6) | async-done | bytes 524320 | tf_op jit(solution)/shard_map/all_to_all | solution.py:23
  286.4 6.5 %all-to-all-start.8 = ((f32[8,128,128]{2,1,0:T(8,128)}), f32[8,128,128]{2,1,0:T(8,128)S(1)}, u32[]{:S(2)}, u32[]{:S(2)}) async-start(f32[8,128,128]{2,1,0:T(8,128)} %bitcast.39), calls=%async_computation.12 | async-start | bytes 1048576 | tf_op jit(solution)/shard_map/all_to_all | solution.py:23
  293.0 12.3 %scatter_custom_fusion.1 = f32[24576,128]{1,0:T(8,128)} fusion(s32[1024]{0:T(1024)S(1)} %bitcast.97, f32[1024,128]{1,0:T(8,128)S(1)} %bitcast.82, f32[]{:T(128)} %constant.80.clone.1), kind=kCustom, calls=%fused_computation.14 | custom fusion | flops 131072 | bytes 12582916 | tf_op jit(solution)/shard_map/scatter-add | solution.py:80
  305.3 15.9 %scatter_fusion = f32[24576,128]{1,0:T(8,128)} fusion(f32[24576,128]{1,0:T(8,128)} %scatter_custom_fusion.1, s32[1024]{0:T(1024)S(1)} %bitcast.96, f32[1024,128]{1,0:T(8,128)S(1)} %bitcast.77), kind=kCustom, calls=%fused_computation.9 | custom fusion | flops 131072 | bytes 1576960 | tf_op jit(solution)/shard_map/scatter-add | solution.py:80
  321.2 15.9 %scatter_fusion.1 = f32[24576,128]{1,0:T(8,128)} fusion(f32[24576,128]{1,0:T(8,128)} %scatter_fusion, s32[1024]{0:T(1024)S(1)} %bitcast.95, f32[1024,128]{1,0:T(8,128)S(1)} %bitcast.78), kind=kCustom, calls=%fused_computation.11 | custom fusion | flops 131072 | bytes 1576960 | tf_op jit(solution)/shard_map/scatter-add | solution.py:80
  337.1 2.5 copy.11
  339.6 30.0 %reduce-scatter.11.cloned.1.call-done = f32[64,512]{1,0:T(8,128)} async-done(((f32[512,512]{1,0:T(8,128)}), f32[64,512]{1,0:T(8,128)}) %reduce-scatter.11.cloned.1.call-update) | async-done | bytes 131088 | tf_op jit(solution)/shard_map/reduce_scatter | solution.py:89
  (55 shorter events, 1.0 us)
Async XLA Ops:
  7.2 47.9 %all-gather.6.cloned.1.call-start = ((), (), s32[]{:S(2)}) async-start(), calls=%async_computation.14 | async-start | bytes 2621440 | tf_op jit(solution)/shard_map/all_gather | solution.py:33
  7.9 104.2 %all-gather.4.cloned.1.call-start = ((), (), s32[]{:S(2)}) async-start(), calls=%async_computation.13 | async-start | bytes 5242880 | tf_op jit(solution)/shard_map/all_gather | solution.py:32
  8.6 116.9 %all-gather.8.cloned.1.call-start = ((), (), s32[]{:S(2)}) async-start(), calls=%async_computation.15 | async-start | bytes 6291456 | tf_op jit(solution)/shard_map/all_gather | solution.py:36
  68.2 32.5 %all-to-all-start.4 = ((s32[8,1,128]{2,1,0:T(1,128)}), s32[8,1,128]{2,1,0:T(1,128)S(1)}, u32[]{:S(2)}, u32[]{:S(2)}) async-start(s32[8,1,128]{2,1,0:T(1,128)} %bitcast.17), calls=%async_computation.5 | async-start | bytes 8192 | tf_op jit(solution)/shard_map/all_to_all | solution.py:15
  100.7 33.2 %all-to-all-start = ((s32[8,1,128]{2,1,0:T(1,128)}), s32[8,1,128]{2,1,0:T(1,128)S(1)}, u32[]{:S(2)}, u32[]{:S(2)}) async-start(s32[8,1,128]{2,1,0:T(1,128)} %bitcast.4), calls=%async_computation.1 | async-start | bytes 8192 | tf_op jit(solution)/shard_map/all_to_all | solution.py:15
  105.6 78.3 %reduce-scatter.5.cloned.1.call-start = ((), (), s32[]{:S(2)}) async-start(), calls=%async_computation.16 | async-start | bytes 1310720 | tf_op jit(solution)/shard_map/reduce_scatter | solution.py:44
  133.0 51.0 %copy-start.1 = (bf16[512,128]{1,0:T(8,128)(2,1)S(1)}, bf16[512,128]{1,0:T(8,128)(2,1)}, u32[]{:S(2)}) copy-start(bf16[512,128]{1,0:T(8,128)(2,1)} %param.15) | copy-start | bytes 393220
  133.9 11.8 %all-to-all-start.2 = ((s32[8,1,128]{2,1,0:T(1,128)}), s32[8,1,128]{2,1,0:T(1,128)S(1)}, u32[]{:S(2)}, u32[]{:S(2)}) async-start(s32[8,1,128]{2,1,0:T(1,128)} %bitcast.11), calls=%async_computation.3 | async-start | bytes 8192 | tf_op jit(solution)/shard_map/all_to_all | solution.py:15
  145.7 12.5 %all-to-all-start.5 = ((bf16[8,128,128]{2,1,0:T(8,128)(2,1)}), bf16[8,128,128]{2,1,0:T(8,128)(2,1)S(1)}, u32[]{:S(2)}, u32[]{:S(2)}) async-start(bf16[8,128,128]{2,1,0:T(8,128)(2,1)} %broadcast_select_fusion), calls=%async_computation.6 | async-start | bytes 524288 | tf_op jit(solution)/shard_map/all_to_all | solution.py:19
  158.2 11.6 %all-to-all-start.1 = ((bf16[8,128,128]{2,1,0:T(8,128)(2,1)}), bf16[8,128,128]{2,1,0:T(8,128)(2,1)S(1)}, u32[]{:S(2)}, u32[]{:S(2)}) async-start(bf16[8,128,128]{2,1,0:T(8,128)(2,1)} %broadcast_select_fusion.2), calls=%async_computation.2 | async-start | bytes 524288 | tf_op jit(solution)/shard_map/all_to_all | solution.py:19
  169.8 12.7 %all-to-all-start.3 = ((bf16[8,128,128]{2,1,0:T(8,128)(2,1)}), bf16[8,128,128]{2,1,0:T(8,128)(2,1)S(1)}, u32[]{:S(2)}, u32[]{:S(2)}) async-start(bf16[8,128,128]{2,1,0:T(8,128)(2,1)} %broadcast_select_fusion.1), calls=%async_computation.4 | async-start | bytes 524288 | tf_op jit(solution)/shard_map/all_to_all | solution.py:19
  176.3 44.9 %reduce-scatter.7.cloned.1.call-start = ((), (), s32[]{:S(2)}) async-start(), calls=%async_computation.17 | async-start | bytes 12582912 | tf_op jit(solution)/shard_map/reduce_scatter | solution.py:99
  204.5 16.7 %copy-start = (f32[512,128]{1,0:T(8,128)S(1)}, f32[512,128]{1,0:T(8,128)}, u32[]{:S(2)}) copy-start(f32[512,128]{1,0:T(8,128)} %reduce-scatter.5.cloned.1.call-done) | copy-start | bytes 786436
  204.5 132.5 %reduce-scatter.9.cloned.1.call-start = ((), (), s32[]{:S(2)}) async-start(), calls=%async_computation.18 | async-start | bytes 5242880 | tf_op jit(solution)/shard_map/reduce_scatter | solution.py:107
  223.8 28.2 %all-to-all-start.7 = ((f32[8,128,128]{2,1,0:T(8,128)}), f32[8,128,128]{2,1,0:T(8,128)S(1)}, u32[]{:S(2)}, u32[]{:S(2)}) async-start(f32[8,128,128]{2,1,0:T(8,128)} %bitcast.33), calls=%async_computation.11 | async-start | bytes 1048576 | tf_op jit(solution)/shard_map/all_to_all | solution.py:23
  228.9 140.6 %reduce-scatter.11.cloned.1.call-start = ((), (), s32[]{:S(2)}) async-start(), calls=%async_computation.19 | async-start | bytes 1179648 | tf_op jit(solution)/shard_map/reduce_scatter | solution.py:89
  252.1 34.4 %all-to-all-start.6 = ((f32[8,128,128]{2,1,0:T(8,128)}), f32[8,128,128]{2,1,0:T(8,128)S(1)}, u32[]{:S(2)}, u32[]{:S(2)}) async-start(f32[8,128,128]{2,1,0:T(8,128)} %bitcast.27), calls=%async_computation.10 | async-start | bytes 1048576 | tf_op jit(solution)/shard_map/all_to_all | solution.py:23
  286.4 34.8 %all-to-all-start.8 = ((f32[8,128,128]{2,1,0:T(8,128)}), f32[8,128,128]{2,1,0:T(8,128)S(1)}, u32[]{:S(2)}, u32[]{:S(2)}) async-start(f32[8,128,128]{2,1,0:T(8,128)} %bitcast.39), calls=%async_computation.12 | async-start | bytes 1048576 | tf_op jit(solution)/shard_map/all_to_all | solution.py:23
Sparse Core Ops, SparseCore 0:
  9.6 45.4 all-gather.5
  56.9 53.0 all-gather.3
  111.6 13.9 all-gather.7
  133.1 28.6 reduce-scatter.4
  204.6 16.4 reduce-scatter.6
  223.3 110.7 reduce-scatter.8
  337.0 32.4 reduce-scatter.10
where the time goes:
time: 381 us; the launch traced here: 376 us
  waiting for transfers between devices  159 us (42%)
  other arithmetic  59.3 us (16%)
  starting transfers between devices  52.3 us (14%)
  blocking collectives  37.9 us (10%)
  local copies, waits for them, and re-layouts  35.8 us (9%)
  matrix products  17.3 us (5%)
  between operations  14.4 us (4%)
    all_gather x1, waiting for transfers between devices, shards(): half_rows = lax.all_gather(w_in, 'dp', axis=0, tiled=True)  46.4 us
    scatter-add x3, other arithmetic, shards(): code_total.at[asked_list[level_index].reshape(-1)]  44.1 us
    all_to_all x3, waiting for transfers between devices, send_sums(): lax.all_to_all(outgoing, ('section', 'dp'), split_axis=0, concat_axis=0,...  42.5 us
    reduce_scatter x1, waiting for transfers between devices, shards(): lax.psum_scatter(lax.dot_general(grad_full, hidden, (((0,), (0,)), ((), (...  30 us
    all_gather x1, blocking collectives, shards(): out_full = lax.all_gather(w_out, ('section', 'dp'), axis=0, tiled=True)  27.1 us
    all_to_all x3, starting transfers between devices, send_sums(): lax.all_to_all(outgoing, ('section', 'dp'), split_axis=0, concat_axis=0,...  19.9 us
    gather x3, local copies, waits for them, and re-layouts, shards(): rows_back = send_rows(jnp.take(flat_book, asked_rows, axis=0))  19.6 us
    all_to_all x3, starting transfers between devices, send_rows(): lax.all_to_all(outgoing, ('section', 'dp'), split_axis=0, concat_axis=0,...  16.8 us
  transfers between devices with their start and end apart: 16, of which 8 were waited for; matrix products, arithmetic and copies ran while one was open for 27% of the time, Pallas kernels for 0%

commit v1 on v0

v1 whole, which is shorter than its diff:
```python
import functools

import jax
import jax.numpy as jnp
from jax import lax
from jax.experimental import pallas as pl
from jax.experimental.pallas import tpu as pltpu
from jax.sharding import PartitionSpec as P

BETA = 0.25
F32 = jnp.float32
BF16 = jnp.bfloat16


def partner_pairs(size, step):
    if size & (size - 1) == 0:
        return [(k, k ^ step) for k in range(size)]
    return [(k, (k + step) % size) for k in range(size)]


def source_of(me, size, step):
    if size & (size - 1) == 0:
        return me ^ step
    return (me + size - step) % size


def target_of(me, size, step):
    if size & (size - 1) == 0:
        return me ^ step
    return (me + step) % size


def shift(value, axis, step):
    return lax.ppermute(value, axis, partner_pairs(lax.axis_size(axis), step))


def sums_kernel(rows_ref, values_ref, out_ref):
    tile = out_ref.shape[1]
    slots = rows_ref.shape[2]
    first = pl.program_id(1) * tile
    row_ids = first + lax.broadcasted_iota(jnp.int32, (tile, slots), 0)
    chosen = jnp.where(row_ids == rows_ref[0], 1.0, 0.0).astype(BF16)
    out_ref[0] = jnp.dot(chosen, values_ref[0], preferred_element_type=F32)


def sum_rows(rows, values, rows_own):
    levels, slots = rows.shape
    width = values.shape[2]
    tile = min(512, rows_own)
    return pl.pallas_call(
        sums_kernel,
        grid=(levels, rows_own // tile),
        in_specs=[
            pl.BlockSpec((1, 1, slots), lambda level, part: (level, 0, 0)),
            pl.BlockSpec((1, slots, width), lambda level, part: (level, 0, 0)),
        ],
        out_specs=pl.BlockSpec((1, tile, width), lambda level, part: (level, part, 0)),
        out_shape=jax.ShapeDtypeStruct((levels, rows_own, width), F32),
        compiler_params=pltpu.CompilerParams(vmem_limit_bytes=24 * 2**20),
        cost_estimate=pl.CostEstimate(
            flops=2 * levels * rows_own * slots * width,
            bytes_accessed=4 * levels * rows_own * width,
            transcendentals=0,
        ),
    )(rows.reshape(levels, 1, slots), values)


def shards(features, w_in, w_out, codebook, codes, decoder_grad):
    n_sec, n_dp, n_mp = (lax.axis_size(a) for a in ("section", "dp", "mp"))
    sec, dp, mp = (lax.axis_index(a) for a in ("section", "dp", "mp"))
    owners = n_sec * n_dp
    me = sec * n_dp + dp
    items, in_part = features.shape
    in_rows, hid = w_in.shape
    out_rows = w_out.shape[0]
    levels, rows_own, width = codebook.shape
    capacity = max(2, 2 * items // owners)
    slots = owners * capacity
    items_all = items * owners

    w_parts = [(dp, w_in, w_out)]
    f_parts = [(mp, features)]
    for step in range(1, n_dp):
        w_parts.append((source_of(dp, n_dp, step), shift(w_in, "dp", step), shift(w_out, "dp", step)))
    for step in range(1, n_mp):
        f_parts.append((source_of(mp, n_mp, step), shift(features, "mp", step)))
    blocks = [(sec * n_dp + at, a, b) for at, a, b in w_parts]
    for step in range(1, n_sec):
        from_sec = source_of(sec, n_sec, step)
        blocks += [
            (from_sec * n_dp + at, shift(a, "section", step), shift(b, "section", step))
            for at, a, b in w_parts
        ]
    w_full = jnp.zeros((owners * in_rows, hid), BF16)
    out_full = jnp.zeros((owners * out_rows, hid), BF16)
    for at, a, b in blocks:
        w_full = lax.dynamic_update_slice(w_full, a, (at * in_rows, 0))
        out_full = lax.dynamic_update_slice(out_full, b, (at * out_rows, 0))
    f_full = jnp.zeros((items, n_mp * in_part), BF16)
    for at, a in f_parts:
        f_full = lax.dynamic_update_slice(f_full, a, (0, at * in_part))

    exchange = functools.partial(
        lax.all_to_all, axis_name=("section", "dp"), split_axis=0, concat_axis=0, tiled=True
    )
    all_codes = exchange(jnp.broadcast_to(codes[None], (owners, levels, items)))
    mine = all_codes // rows_own == me
    before = jnp.arange(items)[:, None] < jnp.arange(items)[None, :]
    place = jnp.dot(
        mine.reshape(-1, items).astype(BF16), before.astype(BF16), preferred_element_type=F32
    ).astype(jnp.int32).reshape(owners, levels, items)
    place = jnp.where(mine, place, capacity)
    local = all_codes % rows_own
    hit = place[:, :, None, :] == jnp.arange(capacity)[None, None, :, None]
    asked = jnp.sum(jnp.where(hit, local[:, :, None, :], 0), axis=3)
    book = codebook.reshape(levels * rows_own, width)
    flat_asked = asked + (jnp.arange(levels) * rows_own)[None, :, None]
    answers = exchange(jnp.take(book, flat_asked, axis=0, mode="clip"))
    owner_of = codes // rows_own
    same = (owner_of[:, :, None] == owner_of[:, None, :]) & before.T[None]
    ranking = jnp.sum(same.astype(jnp.int32), axis=2)
    level_ids = jnp.arange(levels, dtype=jnp.int32)[:, None]
    codewords = jnp.take(
        answers.reshape(owners * levels * capacity, width),
        (owner_of * levels + level_ids) * capacity + ranking,
        axis=0,
        mode="clip",
    )

    preact = jnp.dot(f_full, w_full, preferred_element_type=F32)
    hidden = jax.nn.silu(preact).astype(BF16)
    latent = None
    for step in list(range(1, n_mp)) + [0]:
        goes_to = target_of(mp, n_mp, step)
        rows = lax.dynamic_slice(out_full, (goes_to * width, 0), (width, hid))
        part = lax.dot_general(hidden, rows, (((1,), (1,)), ((), ())), preferred_element_type=F32)
        part = shift(part, "mp", step) if step else part
        latent = part if latent is None else latent + part

    residual = latent
    pull_sum = jnp.zeros_like(latent)
    inputs = []
    for level in range(levels):
        inputs.append(residual.astype(BF16))
        residual = residual - codewords[level].astype(F32)
        pull_sum = pull_sum + residual
    latent_grad = (
        (decoder_grad.astype(F32) + 2.0 * BETA * pull_sum) / jnp.sqrt(F32(items_all))
    ).astype(BF16)

    grad_full = jnp.zeros((items, n_mp * width), BF16)
    for step in range(n_mp):
        got = shift(latent_grad, "mp", step) if step else latent_grad
        at = source_of(mp, n_mp, step) if step else mp
        grad_full = lax.dynamic_update_slice(grad_full, got, (0, at * width))

    slot_of = owner_of * capacity + ranking
    pick = (jnp.arange(slots)[None, :, None] == slot_of[:, None, :]).astype(BF16)
    outgoing = lax.dot_general(
        pick, jnp.stack(inputs), (((2,), (1,)), ((0,), (0,))), preferred_element_type=F32
    ).astype(BF16)
    outgoing = outgoing.reshape(levels, owners, capacity, width).transpose(1, 0, 2, 3)
    incoming = exchange(outgoing)
    code_sums = sum_rows(
        asked.transpose(1, 0, 2).reshape(levels, slots),
        incoming.transpose(1, 0, 2, 3).reshape(levels, slots, width),
        rows_own,
    )

    back_hidden = jnp.dot(grad_full, out_full, preferred_element_type=F32)
    logistic = jax.nn.sigmoid(preact)
    slope = logistic * (1.0 + preact * (1.0 - logistic))
    pre_grad = (back_hidden * slope).astype(BF16)
    over_items = functools.partial(
        lax.dot_general, dimension_numbers=(((0,), (0,)), ((), ())), preferred_element_type=F32
    )

    def in_chunk(at):
        return over_items(lax.dynamic_slice(f_full, (0, at * in_rows), (items, in_rows)), pre_grad)

    def out_chunk(at):
        return over_items(lax.dynamic_slice(grad_full, (0, at * out_rows), (items, out_rows)), hidden)

    def scattered(chunk):
        total = None
        for step in list(range(n_dp - 1, 0, -1)) + [0]:
            goes_to = target_of(dp, n_dp, step) if step else dp
            pair = None
            for other in list(range(1, n_sec)) + [0]:
                to_sec = target_of(sec, n_sec, other) if other else sec
                part = chunk(to_sec * n_dp + goes_to)
                if other:
                    part = shift(part.astype(BF16), "section", other).astype(F32)
                pair = part if pair is None else pair + part
            if step:
                pair = shift(pair.astype(BF16), "dp", step).astype(F32)
            total = pair if total is None else total + pair
        return total

    out_grad = scattered(out_chunk)
    in_grad = scattered(in_chunk)
    return (in_grad, out_grad, code_sums)


def solution(mesh):
    owned = P(("section", "dp"), "mp")
    book = P(None, ("section", "dp"), "mp")
    return jax.shard_map(
        shards,
        mesh=mesh,
        in_specs=(owned, owned, owned, book, P(None, ("section", "dp")), owned),
        out_specs=(owned, owned, book),
        check_vma=False,
    )
```

time: 381 us -> 271 us (0.71)
  other arithmetic: 59.3 us -> 2.89 us
  waiting for transfers between devices: 159 us -> 121 us
  blocking collectives: 37.9 us -> 0 us
  Pallas kernels: 0 us -> 27.9 us
  between operations: 14.4 us -> 1.24 us
  matrix products: 17.3 us -> 28.5 us
  starting transfers between devices: 52.3 us -> 45.8 us
  local copies, waits for them, and re-layouts: 35.8 us -> 41.9 us
    ppermute x0 -> x37, waiting for transfers between devices: none -> 121 us  [shift(): return lax.ppermute(value, axis, partner_pairs(lax.axis_size(axis), step))]
    all_gather x3 -> x0, waiting for transfers between devices: 59.9 us -> none  [the longest x1 46.4 us: shards(): half_rows = lax.all_gather(w_in, 'dp', axis=0, tiled=True)]
    all_to_all x9 -> x3, waiting for transfers between devices: 51.5 us -> 0.01 us  [the longest x1 0.01 us: shards(): all_codes = exchange(jnp.broadcast_to(codes[None], (owners, levels, items)))]
    reduce_scatter x4 -> x0, waiting for transfers between devices: 46.6 us -> none  [the longest x1 30 us: shards(): lax.psum_scatter(lax.dot_general(grad_full, hidden, (((0,), (0,)), ((), (...]
    scatter-add x3 -> x0, other arithmetic: 44.1 us -> none  [shards(): code_total.at[asked_list[level_index].reshape(-1)]]
    all_gather x2 -> x0, blocking collectives: 37.9 us -> none  [the longest x1 27.1 us: shards(): out_full = lax.all_gather(w_out, ('section', 'dp'), axis=0, tiled=True)]
    all_to_all x9 -> x3, starting transfers between devices: 52.2 us -> 15.3 us  [the longest x1 5.28 us: shards(): all_codes = exchange(jnp.broadcast_to(codes[None], (owners, levels, items)))]
    ppermute x0 -> x37, starting transfers between devices: none -> 30.4 us  [shift(): return lax.ppermute(value, axis, partner_pairs(lax.axis_size(axis), step))]
  transfers between devices with their start and end apart: 16 -> 40, of which waited for: 8 -> 10; matrix products, arithmetic and copies ran while one was open for 27% -> 27% of each run, Pallas kernels for 0% -> 0%
where the time goes in v1:
time: 271 us; the launch traced here: 270 us
  waiting for transfers between devices  121 us (45%)
  starting transfers between devices  45.8 us (17%)
  local copies, waits for them, and re-layouts  41.9 us (15%)
  matrix products  28.5 us (11%)
  Pallas kernels  27.9 us (10%)
  other arithmetic  2.89 us (1%)
    ppermute x37, waiting for transfers between devices, shift(): return lax.ppermute(value, axis, partner_pairs(lax.axis_size(axis), step))  121 us
    ppermute x37, starting transfers between devices, shift(): return lax.ppermute(value, axis, partner_pairs(lax.axis_size(axis), step))  30.4 us
    pallas_call x1, Pallas kernels, sum_rows(): pl.pallas_call(sums_kernel, grid=(levels, rows_own // tile), in_specs=[pl...  27.9 us
    gather x1, local copies, waits for them, and re-layouts, shards(): answers = exchange(jnp.take(book, flat_asked, axis=0, mode='clip'))  14.6 us
    dot_general x8, matrix products, in_chunk(): over_items(lax.dynamic_slice(f_full, (0, at * in_rows), (items, in_rows))...  13.1 us
    dynamic_update_slice x8, local copies, waits for them, and re-layouts, shards(): w_full = lax.dynamic_update_slice(w_full, a, (at * in_rows, 0))  9.88 us
    dot_general x1, matrix products, shards(): preact = jnp.dot(f_full, w_full, preferred_element_type=F32)  6.84 us
  transfers between devices with their start and end apart: 40, of which 10 were waited for; matrix products, arithmetic and copies ran while one was open for 27% of the time, Pallas kernels for 0%

profile of v1, /device:TPU:8, one launch (start us, length us, event | category | flops | bytes accessed | tf_op | source)
XLA Modules:
  0.0 269.6 jit_solution(14990579632454969824)
XLA Ops:
  0.7 3.0 %collective-permute-start.4 = (bf16[512,512]{1,0:T(8,128)(2,1)}, bf16[512,512]{1,0:T(8,128)(2,1)}, u32[]{:S(2)}, u32[]{:S(2)}) collective-permute-start(bf16[512,512]{1,0:T(8,128)(2,1)} %param.7), channel_id=1, source_target_pairs={{0,8},{4,12},{8,0},{12,4},{1,9},{5,13},{9,1},{13,5},{2,10},{6,14},... | collective-permute-start | bytes 1572872 | tf_op jit(solution)/shard_map/ppermute | solution.py:34
  4.2 1.1 collective-permute-start.10
  5.3 2.4 collective-permute-start.11
  7.7 1.3 broadcast_in_dim.30
  9.0 5.3 %all-to-all-start = ((s32[8,3,512]{2,1,0:T(4,128)}), s32[8,3,512]{2,1,0:T(4,128)S(1)}, u32[]{:S(2)}, u32[]{:S(2)}) async-start(s32[8,3,512]{2,1,0:T(4,128)} %broadcast_in_dim.30), calls=%async_computation | async-start | bytes 131072 | tf_op jit(solution)/shard_map/all_to_all | solution.py:106
  16.2 2.2 broadcast_in_dim.28
  19.5 2.5 broadcast_in_dim.27
  23.0 16.7 %collective-permute-done.10 = bf16[64,512]{1,0:T(8,128)(2,1)S(1)} collective-permute-done((bf16[64,512]{1,0:T(8,128)(2,1)}, bf16[64,512]{1,0:T(8,128)(2,1)S(1)}, u32[]{:S(2)}, u32[]{:S(2)}) %collective-permute-start.10) | collective-permute-done | bytes 65568 | tf_op jit(solution)/shard_map/ppermute | solution.py:34
  39.7 1.5 collective-permute-start.12
  41.2 13.5 %collective-permute-done.11 = bf16[64,512]{1,0:T(8,128)(2,1)S(1)} collective-permute-done((bf16[64,512]{1,0:T(8,128)(2,1)}, bf16[64,512]{1,0:T(8,128)(2,1)S(1)}, u32[]{:S(2)}, u32[]{:S(2)}) %collective-permute-start.11) | collective-permute-done | bytes 65568 | tf_op jit(solution)/shard_map/ppermute | solution.py:34
  54.8 1.8 collective-permute-done.12
  59.1 14.6 %gather_fusion = bf16[3072,128]{1,0:T(8,128)(2,1)} fusion(bf16[24576,128]{1,0:T(8,128)(2,1)} %bitcast.49, s32[3072]{0:T(1024)S(1)} %broadcast_clamp_fusion), kind=kCustom, calls=%fused_computation | custom fusion | bytes 1585152 | tf_op jit(solution)/shard_map/jit(_take)/gather | solution.py:118
  73.7 5.0 %all-to-all-start.1 = ((bf16[8,3,128,128]{3,2,1,0:T(8,128)(2,1)}), bf16[8,3,128,128]{3,2,1,0:T(8,128)(2,1)S(1)}, u32[]{:S(2)}, u32[]{:S(2)}) async-start(bf16[8,3,128,128]{3,2,1,0:T(8,128)(2,1)} %bitcast.2), calls=%async_computation.1 | async-start | bytes 1572864 | tf_op jit(solution)/shard_map/all_to_all | solution.py:118
  78.7 1.5 collective-permute-start
  81.0 1.6 collective-permute-start.1
  85.4 1.9 constant_dynamic-update-slice_fusion.18
  87.3 1.9 constant_dynamic-update-slice_fusion.17
  89.2 1.9 constant_dynamic-update-slice_fusion.16
  93.6 11.1 %collective-permute-done = bf16[512,1024]{1,0:T(8,128)(2,1)S(1)} collective-permute-done((bf16[512,1024]{1,0:T(8,128)(2,1)S(1)}, bf16[512,1024]{1,0:T(8,128)(2,1)S(1)}, u32[]{:S(2)}, u32[]{:S(2)}) %collective-permute-start) | collective-permute-done | bytes 1048608 | tf_op jit(solution)/shard_map/ppermute | solution.py:34
  104.7 1.0 constant_dynamic-update-slice_fusion.22
  105.7 22.8 %collective-permute-done.1 = bf16[512,1024]{1,0:T(8,128)(2,1)S(1)} collective-permute-done((bf16[512,1024]{1,0:T(8,128)(2,1)S(1)}, bf16[512,1024]{1,0:T(8,128)(2,1)S(1)}, u32[]{:S(2)}, u32[]{:S(2)}) %collective-permute-start.1) | collective-permute-done | bytes 1048608 | tf_op jit(solution)/shard_map/ppermute | solution.py:34
  129.5 1.0 constant_dynamic-update-slice_fusion.20
  131.4 6.8 %multiply_convert_fusion = (bf16[512,512]{1,0:T(8,128)(2,1)S(1)}, f32[512,512]{1,0:T(8,128)}) fusion(bf16[512,4096]{1,0:T(8,128)(2,1)} %constant_dynamic-update-slice_fusion.20, bf16[4096,512]{1,0:T(8,128)(2,1)} %constant_dynamic-update-slice_fusion.12), kind=kOutput, calls=%fused_computation.27 | convolution fusion | flops 2148794368 | bytes 9961472 | tf_op jit(solution)/shard_map/dot_general | solution.py:130
  138.5 1.6 collective-permute-start.19
  140.4 1.6 collective-permute-start.17
  142.9 3.2 %gather_fusion.1 = bf16[1536,128]{1,0:T(8,128)(2,1)S(1)} fusion(bf16[3072,128]{1,0:T(8,128)(2,1)S(1)} %bitcast.48, s32[2048]{0:T(1024)S(1)} %pad_clamp_fusion), kind=kCustom, calls=%fused_computation.1 | custom fusion | bytes 792576 | tf_op jit(solution)/shard_map/jit(_take)/gather | solution.py:123
  146.1 2.6 collective-permute-done.19
  148.7 3.9 %collective-permute-done.17 = f32[512,128]{1,0:T(8,128)} collective-permute-done((f32[512,128]{1,0:T(8,128)S(1)}, f32[512,128]{1,0:T(8,128)}, u32[]{:S(2)}, u32[]{:S(2)}) %collective-permute-start.17) | collective-permute-done | bytes 262176 | tf_op jit(solution)/shard_map/ppermute | solution.py:34
  152.6 1.4 constant_dynamic-update-slice_fusion.3
  154.6 1.4 collective-permute-start.21
  156.0 1.5 collective-permute-start.22
  157.6 1.2 fusion.2
  159.8 5.1 %all-to-all-start.2 = ((bf16[8,3,128,128]{3,2,1,0:T(8,128)(2,1)}), bf16[8,3,128,128]{3,2,1,0:T(8,128)(2,1)S(1)}, u32[]{:S(2)}, u32[]{:S(2)}) async-start(bf16[8,3,128,128]{3,2,1,0:T(8,128)(2,1)} %bitcast.45), calls=%async_computation.2 | async-start | bytes 1572864 | tf_op jit(solution)/shard_map/all_to_all | solution.py:163
  165.0 1.8 fusion.3
  166.9 1.5 convolution_convert_fusion
  168.4 1.5 convolution_convert_fusion.1
  169.9 1.5 convolution_convert_fusion.2
  171.4 1.5 convolution_convert_fusion.3
  176.4 1.9 collective-permute-done.32
  179.2 1.5 add_convert_fusion
  181.0 1.5 add_convert_fusion.1
  182.5 2.8 %collective-permute-start.33 = (bf16[64,512]{1,0:T(8,128)(2,1)S(1)}, bf16[64,512]{1,0:T(8,128)(2,1)S(1)}, u32[]{:S(2)}, u32[]{:S(2)}) collective-permute-start(bf16[64,512]{1,0:T(8,128)(2,1)S(1)} %add_convert_fusion.4), channel_id=1, source_target_pairs={{0,8},{4,12},{8,0},{12,4},{1,9},{5,13},{9,1},{13,5},{2,10},{6,14},... | collective-permute-start | bytes 196616 | tf_op jit(solution)/shard_map/ppermute | solution.py:34
  185.3 1.5 add_convert_fusion.2
  186.8 1.5 collective-permute-start.28
  188.9 1.5 collective-permute-start.24
  191.3 46.7 %collective-permute-done.31 = bf16[64,512]{1,0:T(8,128)(2,1)S(1)} collective-permute-done((bf16[64,512]{1,0:T(8,128)(2,1)S(1)}, bf16[64,512]{1,0:T(8,128)(2,1)S(1)}, u32[]{:S(2)}, u32[]{:S(2)}) %collective-permute-start.31) | collective-permute-done | bytes 65568 | tf_op jit(solution)/shard_map/ppermute | solution.py:34
  239.1 2.6 add_add_fusion
  241.7 27.9 %shard_map.85 = f32[3,8192,128]{2,1,0:T(8,128)} custom-call(s32[3,1,1024]{2,1,0:T(1,128)S(1)} %bitcast.47, bf16[3,1024,128]{2,1,0:T(8,128)(2,1)S(1)} %bitcast.46), custom_call_target="tpu_custom_call" | custom-call | flops 6442450944 | bytes 12582912 | tf_op jit(solution)/shard_map/pallas_call | solution.py:50
  (118 shorter events, 25.2 us)
Async XLA Ops:
  0.6 17.8 %copy-start.1 = (bf16[512,512]{1,0:T(8,128)(2,1)S(1)}, bf16[512,512]{1,0:T(8,128)(2,1)}, u32[]{:S(2)}) copy-start(bf16[512,512]{1,0:T(8,128)(2,1)} %param.7) | copy-start | bytes 1572868
  0.6 18.7 %copy-start.4 = (bf16[64,512]{1,0:T(8,128)(2,1)S(1)}, bf16[64,512]{1,0:T(8,128)(2,1)}, u32[]{:S(2)}) copy-start(bf16[64,512]{1,0:T(8,128)(2,1)} %param.8) | copy-start | bytes 196612
  0.7 80.4 %collective-permute-start.3 = (bf16[512,512]{1,0:T(8,128)(2,1)}, bf16[512,512]{1,0:T(8,128)(2,1)}, u32[]{:S(2)}, u32[]{:S(2)}) collective-permute-start(bf16[512,512]{1,0:T(8,128)(2,1)} %param.7), channel_id=1, source_target_pairs={{0,4},{4,0},{8,12},{12,8},{1,5},{5,1},{9,13},{13,9},{2,6},{6,2},{1... | collective-permute-start | bytes 1572872 | tf_op jit(solution)/shard_map/ppermute | solution.py:34
  0.7 82.7 %collective-permute-start.4 = (bf16[512,512]{1,0:T(8,128)(2,1)}, bf16[512,512]{1,0:T(8,128)(2,1)}, u32[]{:S(2)}, u32[]{:S(2)}) collective-permute-start(bf16[512,512]{1,0:T(8,128)(2,1)} %param.7), channel_id=1, source_target_pairs={{0,8},{4,12},{8,0},{12,4},{1,9},{5,13},{9,1},{13,5},{2,10},{6,14},... | collective-permute-start | bytes 1572872 | tf_op jit(solution)/shard_map/ppermute | solution.py:34
  3.8 80.2 %collective-permute-start.5 = (bf16[512,512]{1,0:T(8,128)(2,1)}, bf16[512,512]{1,0:T(8,128)(2,1)}, u32[]{:S(2)}, u32[]{:S(2)}) collective-permute-start(bf16[512,512]{1,0:T(8,128)(2,1)} %param.7), channel_id=1, source_target_pairs={{0,12},{4,8},{8,4},{12,0},{1,13},{5,9},{9,5},{13,1},{2,14},{6,10},... | collective-permute-start | bytes 1572872 | tf_op jit(solution)/shard_map/ppermute | solution.py:34
  4.2 35.5 %collective-permute-start.10 = (bf16[64,512]{1,0:T(8,128)(2,1)}, bf16[64,512]{1,0:T(8,128)(2,1)S(1)}, u32[]{:S(2)}, u32[]{:S(2)}) collective-permute-start(bf16[64,512]{1,0:T(8,128)(2,1)} %param.8), channel_id=1, source_target_pairs={{0,4},{4,0},{8,12},{12,8},{1,5},{5,1},{9,13},{13,9},{2,6},{6,2},{1... | collective-permute-start | bytes 196616 | tf_op jit(solution)/shard_map/ppermute | solution.py:34
  5.3 49.4 %collective-permute-start.11 = (bf16[64,512]{1,0:T(8,128)(2,1)}, bf16[64,512]{1,0:T(8,128)(2,1)S(1)}, u32[]{:S(2)}, u32[]{:S(2)}) collective-permute-start(bf16[64,512]{1,0:T(8,128)(2,1)} %param.8), channel_id=1, source_target_pairs={{0,8},{4,12},{8,0},{12,4},{1,9},{5,13},{9,1},{13,5},{2,10},{6,14},... | collective-permute-start | bytes 196616 | tf_op jit(solution)/shard_map/ppermute | solution.py:34
  9.0 48.1 %all-to-all-start = ((s32[8,3,512]{2,1,0:T(4,128)}), s32[8,3,512]{2,1,0:T(4,128)S(1)}, u32[]{:S(2)}, u32[]{:S(2)}) async-start(s32[8,3,512]{2,1,0:T(4,128)} %broadcast_in_dim.30), calls=%async_computation | async-start | bytes 131072 | tf_op jit(solution)/shard_map/all_to_all | solution.py:106
  16.2 5.8 %copy-start = (bf16[512,1024]{1,0:T(8,128)(2,1)S(1)}, bf16[512,1024]{1,0:T(8,128)(2,1)}, u32[]{:S(2)}) copy-start(bf16[512,1024]{1,0:T(8,128)(2,1)} %param.6) | copy-start | bytes 3145732
  39.7 16.9 %collective-permute-start.12 = (bf16[64,512]{1,0:T(8,128)(2,1)S(1)}, bf16[64,512]{1,0:T(8,128)(2,1)S(1)}, u32[]{:S(2)}, u32[]{:S(2)}) collective-permute-start(bf16[64,512]{1,0:T(8,128)(2,1)S(1)} %copy-done.4), channel_id=1, source_target_pairs={{0,12},{4,8},{8,4},{12,0},{1,13},{5,9},{9,5},{13,1},{2,14},{6,10},... | collective-permute-start | bytes 196616 | tf_op jit(solution)/shard_map/ppermute | solution.py:34
  54.7 1.8 collective-permute-start.13
  56.6 1.9 collective-permute-start.14
  56.6 2.0 collective-permute-start.15
  58.5 26.4 %collective-permute-start.6 = (bf16[512,512]{1,0:T(8,128)(2,1)S(1)}, bf16[512,512]{1,0:T(8,128)(2,1)S(1)}, u32[]{:S(2)}, u32[]{:S(2)}) collective-permute-start(bf16[512,512]{1,0:T(8,128)(2,1)S(1)} %copy-done.1), channel_id=1, source_target_pairs={{0,16},{16,0},{1,17},{17,1},{2,18},{18,2},{3,19},{19,3},{4,20},{20... | collective-permute-start | bytes 1572872 | tf_op jit(solution)/shard_map/ppermute | solution.py:34
  58.6 15.1 %copy-start.5 = (bf16[64,512]{1,0:T(8,128)(2,1)}, bf16[64,512]{1,0:T(8,128)(2,1)S(1)}, u32[]{:S(2)}) copy-start(bf16[64,512]{1,0:T(8,128)(2,1)S(1)} %collective-permute-done.15) | copy-start | bytes 196612
  58.6 20.1 %collective-permute-start.16 = (bf16[64,512]{1,0:T(8,128)(2,1)S(1)}, bf16[64,512]{1,0:T(8,128)(2,1)}, u32[]{:S(2)}, u32[]{:S(2)}) collective-permute-start(bf16[64,512]{1,0:T(8,128)(2,1)S(1)} %collective-permute-done.12), channel_id=1, source_target_pairs={{0,16},{16,0},{1,17},{17,1},{2,18},{18,2},{3,19},{19,3},{4,20},{20... | collective-permute-start | bytes 196616 | tf_op jit(solution)/shard_map/ppermute | solution.py:34
  73.7 69.2 %all-to-all-start.1 = ((bf16[8,3,128,128]{3,2,1,0:T(8,128)(2,1)}), bf16[8,3,128,128]{3,2,1,0:T(8,128)(2,1)S(1)}, u32[]{:S(2)}, u32[]{:S(2)}) async-start(bf16[8,3,128,128]{3,2,1,0:T(8,128)(2,1)} %bitcast.2), calls=%async_computation.1 | async-start | bytes 1572864 | tf_op jit(solution)/shard_map/all_to_all | solution.py:118
  78.7 26.0 %collective-permute-start = (bf16[512,1024]{1,0:T(8,128)(2,1)S(1)}, bf16[512,1024]{1,0:T(8,128)(2,1)S(1)}, u32[]{:S(2)}, u32[]{:S(2)}) collective-permute-start(bf16[512,1024]{1,0:T(8,128)(2,1)S(1)} %copy-done), channel_id=1, source_target_pairs={{0,1},{1,0},{2,3},{3,2},{4,5},{5,4},{6,7},{7,6},{8,9},{9,8},{10,11... | collective-permute-start | bytes 3145736 | tf_op jit(solution)/shard_map/ppermute | solution.py:34
  81.0 47.5 %collective-permute-start.1 = (bf16[512,1024]{1,0:T(8,128)(2,1)S(1)}, bf16[512,1024]{1,0:T(8,128)(2,1)S(1)}, u32[]{:S(2)}, u32[]{:S(2)}) collective-permute-start(bf16[512,1024]{1,0:T(8,128)(2,1)S(1)} %copy-done), channel_id=1, source_target_pairs={{0,2},{1,3},{2,0},{3,1},{4,6},{5,7},{6,4},{7,5},{8,10},{9,11},{10,... | collective-permute-start | bytes 3145736 | tf_op jit(solution)/shard_map/ppermute | solution.py:34
  83.4 46.1 %collective-permute-start.2 = (bf16[512,1024]{1,0:T(8,128)(2,1)S(1)}, bf16[512,1024]{1,0:T(8,128)(2,1)S(1)}, u32[]{:S(2)}, u32[]{:S(2)}) collective-permute-start(bf16[512,1024]{1,0:T(8,128)(2,1)S(1)} %copy-done), channel_id=1, source_target_pairs={{0,3},{1,2},{2,1},{3,0},{4,7},{5,6},{6,5},{7,4},{8,11},{9,10},{10,... | collective-permute-start | bytes 3145736 | tf_op jit(solution)/shard_map/ppermute | solution.py:34
  84.0 7.9 %collective-permute-start.7 = (bf16[512,512]{1,0:T(8,128)(2,1)}, bf16[512,512]{1,0:T(8,128)(2,1)S(1)}, u32[]{:S(2)}, u32[]{:S(2)}) collective-permute-start(bf16[512,512]{1,0:T(8,128)(2,1)} %collective-permute-done.3), channel_id=1, source_target_pairs={{0,16},{16,0},{1,17},{17,1},{2,18},{18,2},{3,19},{19,3},{4,20},{20... | collective-permute-start | bytes 1572872 | tf_op jit(solution)/shard_map/ppermute | solution.py:34
  84.8 7.9 %collective-permute-start.8 = (bf16[512,512]{1,0:T(8,128)(2,1)}, bf16[512,512]{1,0:T(8,128)(2,1)S(1)}, u32[]{:S(2)}, u32[]{:S(2)}) collective-permute-start(bf16[512,512]{1,0:T(8,128)(2,1)} %collective-permute-done.4), channel_id=1, source_target_pairs={{0,16},{16,0},{1,17},{17,1},{2,18},{18,2},{3,19},{19,3},{4,20},{20... | collective-permute-start | bytes 1572872 | tf_op jit(solution)/shard_map/ppermute | solution.py:34
  91.9 38.7 %collective-permute-start.9 = (bf16[512,512]{1,0:T(8,128)(2,1)}, bf16[512,512]{1,0:T(8,128)(2,1)S(1)}, u32[]{:S(2)}, u32[]{:S(2)}) collective-permute-start(bf16[512,512]{1,0:T(8,128)(2,1)} %collective-permute-done.5), channel_id=1, source_target_pairs={{0,16},{16,0},{1,17},{17,1},{2,18},{18,2},{3,19},{19,3},{4,20},{20... | collective-permute-start | bytes 1572872 | tf_op jit(solution)/shard_map/ppermute | solution.py:34
  131.4 11.4 %copy-start.3 = (s32[3,512]{1,0:T(4,128)S(1)}, s32[3,512]{1,0:T(4,128)}, u32[]{:S(2)}) copy-start(s32[3,512]{1,0:T(4,128)} %param.10) | copy-start | bytes 18436
  138.2 14.4 %copy-start.2 = (bf16[512,128]{1,0:T(8,128)(2,1)S(1)}, bf16[512,128]{1,0:T(8,128)(2,1)}, u32[]{:S(2)}) copy-start(bf16[512,128]{1,0:T(8,128)(2,1)} %param.11) | copy-start | bytes 393220
  138.5 10.1 %collective-permute-start.19 = (f32[512,128]{1,0:T(8,128)S(1)}, f32[512,128]{1,0:T(8,128)S(1)}, u32[]{:S(2)}, u32[]{:S(2)}) collective-permute-start(f32[512,128]{1,0:T(8,128)S(1)} %fusion.49), channel_id=1, source_target_pairs={{0,3},{1,2},{2,1},{3,0},{4,7},{5,6},{6,5},{7,4},{8,11},{9,10},{10,... | collective-permute-start | bytes 786440 | tf_op jit(solution)/shard_map/ppermute | solution.py:34
  140.4 12.1 %collective-permute-start.17 = (f32[512,128]{1,0:T(8,128)S(1)}, f32[512,128]{1,0:T(8,128)}, u32[]{:S(2)}, u32[]{:S(2)}) collective-permute-start(f32[512,128]{1,0:T(8,128)S(1)} %fusion.53), channel_id=1, source_target_pairs={{0,1},{1,0},{2,3},{3,2},{4,5},{5,4},{6,7},{7,6},{8,9},{9,8},{10,11... | collective-permute-start | bytes 786440 | tf_op jit(solution)/shard_map/ppermute | solution.py:34
  142.3 10.3 %collective-permute-start.18 = (f32[512,128]{1,0:T(8,128)S(1)}, f32[512,128]{1,0:T(8,128)}, u32[]{:S(2)}, u32[]{:S(2)}) collective-permute-start(f32[512,128]{1,0:T(8,128)S(1)} %fusion.51), channel_id=1, source_target_pairs={{0,2},{1,3},{2,0},{3,1},{4,6},{5,7},{6,4},{7,5},{8,10},{9,11},{10,... | collective-permute-start | bytes 786440 | tf_op jit(solution)/shard_map/ppermute | solution.py:34
  154.0 10.9 %collective-permute-start.20 = (bf16[512,128]{1,0:T(8,128)(2,1)S(1)}, bf16[512,128]{1,0:T(8,128)(2,1)S(1)}, u32[]{:S(2)}, u32[]{:S(2)}) collective-permute-start(bf16[512,128]{1,0:T(8,128)(2,1)S(1)} %get-tuple-element.4), channel_id=1, source_target_pairs={{0,1},{1,0},{2,3},{3,2},{4,5},{5,4},{6,7},{7,6},{8,9},{9,8},{10,11... | collective-permute-start | bytes 393224 | tf_op jit(solution)/shard_map/ppermute | solution.py:34
  154.6 10.3 %collective-permute-start.21 = (bf16[512,128]{1,0:T(8,128)(2,1)S(1)}, bf16[512,128]{1,0:T(8,128)(2,1)S(1)}, u32[]{:S(2)}, u32[]{:S(2)}) collective-permute-start(bf16[512,128]{1,0:T(8,128)(2,1)S(1)} %get-tuple-element.4), channel_id=1, source_target_pairs={{0,2},{1,3},{2,0},{3,1},{4,6},{5,7},{6,4},{7,5},{8,10},{9,11},{10,... | collective-permute-start | bytes 393224 | tf_op jit(solution)/shard_map/ppermute | solution.py:34
  156.0 8.9 %collective-permute-start.22 = (bf16[512,128]{1,0:T(8,128)(2,1)S(1)}, bf16[512,128]{1,0:T(8,128)(2,1)S(1)}, u32[]{:S(2)}, u32[]{:S(2)}) collective-permute-start(bf16[512,128]{1,0:T(8,128)(2,1)S(1)} %get-tuple-element.4), channel_id=1, source_target_pairs={{0,3},{1,2},{2,1},{3,0},{4,7},{5,6},{6,5},{7,4},{8,11},{9,10},{10,... | collective-permute-start | bytes 393224 | tf_op jit(solution)/shard_map/ppermute | solution.py:34
  159.8 81.8 %all-to-all-start.2 = ((bf16[8,3,128,128]{3,2,1,0:T(8,128)(2,1)}), bf16[8,3,128,128]{3,2,1,0:T(8,128)(2,1)S(1)}, u32[]{:S(2)}, u32[]{:S(2)}) async-start(bf16[8,3,128,128]{3,2,1,0:T(8,128)(2,1)} %bitcast.45), calls=%async_computation.2 | async-start | bytes 1572864 | tf_op jit(solution)/shard_map/all_to_all | solution.py:163
  173.9 4.9 %collective-permute-start.27 = (bf16[512,512]{1,0:T(8,128)(2,1)S(1)}, bf16[512,512]{1,0:T(8,128)(2,1)S(1)}, u32[]{:S(2)}, u32[]{:S(2)}) collective-permute-start(bf16[512,512]{1,0:T(8,128)(2,1)S(1)} %convolution_convert_fusion.1), channel_id=1, source_target_pairs={{0,16},{16,0},{1,17},{17,1},{2,18},{18,2},{3,19},{19,3},{4,20},{20... | collective-permute-start | bytes 1572872 | tf_op jit(solution)/shard_map/ppermute | solution.py:34
  174.1 1.9 collective-permute-start.34
  174.8 64.3 %collective-permute-start.29 = (bf16[512,512]{1,0:T(8,128)(2,1)S(1)}, bf16[512,512]{1,0:T(8,128)(2,1)S(1)}, u32[]{:S(2)}, u32[]{:S(2)}) collective-permute-start(bf16[512,512]{1,0:T(8,128)(2,1)S(1)} %convolution_convert_fusion), channel_id=1, source_target_pairs={{0,16},{16,0},{1,17},{17,1},{2,18},{18,2},{3,19},{19,3},{4,20},{20... | collective-permute-start | bytes 1572872 | tf_op jit(solution)/shard_map/ppermute | solution.py:34
  175.0 5.8 %collective-permute-start.25 = (bf16[512,512]{1,0:T(8,128)(2,1)S(1)}, bf16[512,512]{1,0:T(8,128)(2,1)S(1)}, u32[]{:S(2)}, u32[]{:S(2)}) collective-permute-start(bf16[512,512]{1,0:T(8,128)(2,1)S(1)} %convolution_convert_fusion.2), channel_id=1, source_target_pairs={{0,16},{16,0},{1,17},{17,1},{2,18},{18,2},{3,19},{19,3},{4,20},{20... | collective-permute-start | bytes 1572872 | tf_op jit(solution)/shard_map/ppermute | solution.py:34
  175.3 7.1 %collective-permute-start.23 = (bf16[512,512]{1,0:T(8,128)(2,1)S(1)}, bf16[512,512]{1,0:T(8,128)(2,1)S(1)}, u32[]{:S(2)}, u32[]{:S(2)}) collective-permute-start(bf16[512,512]{1,0:T(8,128)(2,1)S(1)} %convolution_convert_fusion.3), channel_id=1, source_target_pairs={{0,16},{16,0},{1,17},{17,1},{2,18},{18,2},{3,19},{19,3},{4,20},{20... | collective-permute-start | bytes 1572872 | tf_op jit(solution)/shard_map/ppermute | solution.py:34
  175.9 2.4 collective-permute-start.32
  178.3 8.5 %collective-permute-start.36 = (bf16[64,512]{1,0:T(8,128)(2,1)S(1)}, bf16[64,512]{1,0:T(8,128)(2,1)S(1)}, u32[]{:S(2)}, u32[]{:S(2)}) collective-permute-start(bf16[64,512]{1,0:T(8,128)(2,1)S(1)} %convolution_convert_fusion.4), channel_id=1, source_target_pairs={{0,16},{16,0},{1,17},{17,1},{2,18},{18,2},{3,19},{19,3},{4,20},{20... | collective-permute-start | bytes 196616 | tf_op jit(solution)/shard_map/ppermute | solution.py:34
  178.8 9.6 %collective-permute-start.30 = (bf16[64,512]{1,0:T(8,128)(2,1)S(1)}, bf16[64,512]{1,0:T(8,128)(2,1)S(1)}, u32[]{:S(2)}, u32[]{:S(2)}) collective-permute-start(bf16[64,512]{1,0:T(8,128)(2,1)S(1)} %convolution_convert_fusion.7), channel_id=1, source_target_pairs={{0,16},{16,0},{1,17},{17,1},{2,18},{18,2},{3,19},{19,3},{4,20},{20... | collective-permute-start | bytes 196616 | tf_op jit(solution)/shard_map/ppermute | solution.py:34
  180.7 8.2 %collective-permute-start.35 = (bf16[64,512]{1,0:T(8,128)(2,1)S(1)}, bf16[64,512]{1,0:T(8,128)(2,1)S(1)}, u32[]{:S(2)}, u32[]{:S(2)}) collective-permute-start(bf16[64,512]{1,0:T(8,128)(2,1)S(1)} %add_convert_fusion.3), channel_id=1, source_target_pairs={{0,4},{4,0},{8,12},{12,8},{1,5},{5,1},{9,13},{13,9},{2,6},{6,2},{1... | collective-permute-start | bytes 196616 | tf_op jit(solution)/shard_map/ppermute | solution.py:34
  182.5 8.2 %collective-permute-start.33 = (bf16[64,512]{1,0:T(8,128)(2,1)S(1)}, bf16[64,512]{1,0:T(8,128)(2,1)S(1)}, u32[]{:S(2)}, u32[]{:S(2)}) collective-permute-start(bf16[64,512]{1,0:T(8,128)(2,1)S(1)} %add_convert_fusion.4), channel_id=1, source_target_pairs={{0,8},{4,12},{8,0},{12,4},{1,9},{5,13},{9,1},{13,5},{2,10},{6,14},... | collective-permute-start | bytes 196616 | tf_op jit(solution)/shard_map/ppermute | solution.py:34
  186.8 52.2 %collective-permute-start.28 = (bf16[512,512]{1,0:T(8,128)(2,1)S(1)}, bf16[512,512]{1,0:T(8,128)(2,1)S(1)}, u32[]{:S(2)}, u32[]{:S(2)}) collective-permute-start(bf16[512,512]{1,0:T(8,128)(2,1)S(1)} %add_convert_fusion), channel_id=1, source_target_pairs={{0,4},{4,0},{8,12},{12,8},{1,5},{5,1},{9,13},{13,9},{2,6},{6,2},{1... | collective-permute-start | bytes 1572872 | tf_op jit(solution)/shard_map/ppermute | solution.py:34
  188.4 50.7 %collective-permute-start.26 = (bf16[512,512]{1,0:T(8,128)(2,1)S(1)}, bf16[512,512]{1,0:T(8,128)(2,1)S(1)}, u32[]{:S(2)}, u32[]{:S(2)}) collective-permute-start(bf16[512,512]{1,0:T(8,128)(2,1)S(1)} %add_convert_fusion.1), channel_id=1, source_target_pairs={{0,8},{4,12},{8,0},{12,4},{1,9},{5,13},{9,1},{13,5},{2,10},{6,14},... | collective-permute-start | bytes 1572872 | tf_op jit(solution)/shard_map/ppermute | solution.py:34
  188.9 50.1 %collective-permute-start.24 = (bf16[512,512]{1,0:T(8,128)(2,1)S(1)}, bf16[512,512]{1,0:T(8,128)(2,1)S(1)}, u32[]{:S(2)}, u32[]{:S(2)}) collective-permute-start(bf16[512,512]{1,0:T(8,128)(2,1)S(1)} %add_convert_fusion.2), channel_id=1, source_target_pairs={{0,12},{4,8},{8,4},{12,0},{1,13},{5,9},{9,5},{13,1},{2,14},{6,10},... | collective-permute-start | bytes 1572872 | tf_op jit(solution)/shard_map/ppermute | solution.py:34
  190.7 47.4 %collective-permute-start.31 = (bf16[64,512]{1,0:T(8,128)(2,1)S(1)}, bf16[64,512]{1,0:T(8,128)(2,1)S(1)}, u32[]{:S(2)}, u32[]{:S(2)}) collective-permute-start(bf16[64,512]{1,0:T(8,128)(2,1)S(1)} %add_convert_fusion.5), channel_id=1, source_target_pairs={{0,12},{4,8},{8,4},{12,0},{1,13},{5,9},{9,5},{13,1},{2,14},{6,10},... | collective-permute-start | bytes 196616 | tf_op jit(solution)/shard_map/ppermute | solution.py:34

commit v2 on v1

--- a/solution.py
+++ b/solution.py
@@ -65,6 +65,199 @@
     )(rows.reshape(levels, 1, slots), values)
 
 
+def gather_kernel(
+    f_ref, w_ref, o_ref, ans_ref, f_out, w_out, o_out, ans_out,
+    local_sem, f_send, f_recv, dp_send, dp_recv, sec_send, sec_recv, ans_send, ans_recv,
+):
+    n_dp, n_mp = lax.axis_size("dp"), lax.axis_size("mp")
+    sec, dp, mp = (lax.axis_index(a) for a in ("section", "dp", "mp"))
+    owners = ans_ref.shape[0]
+    me = sec * n_dp + dp
+    base = sec * n_dp
+    other = {"section": 1 - sec}
+    items, in_part = f_ref.shape
+    barrier = pltpu.get_barrier_semaphore()
+
+    def owner_at(step):
+        at = lax.rem(me + step, owners)
+        return at, {"section": at // n_dp, "dp": lax.rem(at, n_dp)}
+
+    for step in range(1, owners):
+        pl.semaphore_signal(barrier, inc=1, device_id=owner_at(step)[1], device_id_type=pl.DeviceIdType.MESH)
+    for step in range(1, n_mp):
+        pl.semaphore_signal(
+            barrier, inc=1, device_id={"mp": target_of(mp, n_mp, step)}, device_id_type=pl.DeviceIdType.MESH
+        )
+    pl.semaphore_wait(barrier, owners - 1 + n_mp - 1)
+
+    def remote(src, dst, send, recv, to):
+        return pltpu.make_async_remote_copy(
+            src_ref=src, dst_ref=dst, send_sem=send, recv_sem=recv,
+            device_id=to, device_id_type=pl.DeviceIdType.MESH,
+        )
+
+    def columns(at):
+        return pl.ds(pl.multiple_of(at * in_part, in_part), in_part)
+
+    answers = []
+    for step in range(1, owners):
+        at, to = owner_at(step)
+        answers.append(remote(ans_ref.at[at], ans_out.at[me], ans_send.at[step], ans_recv.at[step], to))
+        answers[-1].start()
+
+    relay = n_mp == 4
+    feature = [
+        remote(
+            f_ref, f_out.at[:, columns(mp)], f_send.at[step], f_recv.at[step],
+            {"mp": target_of(mp, n_mp, step)},
+        )
+        for step in (range(1, 3) if relay else range(1, n_mp))
+    ]
+
+    def weights(block, src, side, step, to):
+        sems = (dp_send, dp_recv) if side < 2 else (sec_send, sec_recv)
+        place = side if side < 2 else side - 2
+        pairs = ((w_ref, w_out), (o_ref, o_out))
+        return [
+            remote(
+                own if src is None else out.at[src], out.at[block],
+                sems[0].at[place, step, k], sems[1].at[place, step, k], to,
+            )
+            for k, (own, out) in enumerate(pairs)
+        ]
+
+    def start(copies):
+        for copy in copies:
+            copy.start()
+
+    right, left = {"dp": dp + 1}, {"dp": dp - 1}
+
+    @pl.when(dp < n_dp - 1)
+    def _():
+        start(weights(me, None, 0, 0, right))
+
+    @pl.when(dp > 0)
+    def _():
+        start(weights(me, None, 1, 0, left))
+
+    start(feature)
+    own_sec = weights(me, None, 2, n_dp - 1, other)
+    start(own_sec)
+    locals_ = [
+        pltpu.make_async_copy(f_ref, f_out.at[:, columns(mp)], local_sem.at[0]),
+        pltpu.make_async_copy(w_ref, w_out.at[me], local_sem.at[1]),
+        pltpu.make_async_copy(o_ref, o_out.at[me], local_sem.at[2]),
+        pltpu.make_async_copy(ans_ref.at[me], ans_out.at[me], local_sem.at[3]),
+    ]
+    start(locals_)
+
+    def arrive(block, side, step):
+        for copy in weights(block, block, side, step, other):
+            copy.wait_recv()
+
+    halves = []
+    for step in range(n_dp - 1):
+        @pl.when(dp - 1 - step >= 0)
+        def _(step=step):
+            block = base + dp - 1 - step
+            arrive(block, 0, step)
+            if step + 1 < n_dp - 1:
+                @pl.when(dp < n_dp - 1)
+                def _():
+                    start(weights(block, block, 0, step + 1, right))
+            start(weights(block, block, 2, step, other))
+
+        @pl.when(dp + 1 + step <= n_dp - 1)
+        def _(step=step):
+            block = base + dp + 1 + step
+            arrive(block, 1, step)
+            if step + 1 < n_dp - 1:
+                @pl.when(dp > 0)
+                def _():
+                    start(weights(block, block, 1, step + 1, left))
+            start(weights(block, block, 3, step, other))
+
+        if step == 0:
+            for copy in feature:
+                copy.wait_recv()
+            if relay:
+                half = items // 2
+                for k, (source, to) in enumerate(((mp ^ 1, mp ^ 2), (mp ^ 2, mp ^ 1))):
+                    view = f_out.at[pl.ds(k * half, half), columns(source)]
+                    halves.append(remote(view, view, f_send.at[3 + k], f_recv.at[3 + k], {"mp": to}))
+                start(halves)
+
+    for copy in locals_ + answers:
+        copy.wait()
+    for copy in feature:
+        copy.wait_send()
+    if relay:
+        for k in range(2):
+            view = f_out.at[pl.ds(k * (items // 2), items // 2), columns(mp ^ 3)]
+            remote(view, view, f_send.at[3 + k], f_recv.at[3 + k], {"mp": mp ^ 1}).wait_recv()
+            halves[k].wait_send()
+    elsewhere = (1 - sec) * n_dp
+    for copy in own_sec:
+        copy.wait_send()
+    arrive(elsewhere + dp, 2, n_dp - 1)
+
+    def sent(block, side, step):
+        for copy in weights(block, block, side, step, other):
+            copy.wait_send()
+
+    @pl.when(dp < n_dp - 1)
+    def _():
+        sent(me, 0, 0)
+
+    @pl.when(dp > 0)
+    def _():
+        sent(me, 1, 0)
+
+    for step in range(n_dp - 1):
+        @pl.when(dp - 1 - step >= 0)
+        def _(step=step):
+            if step + 1 < n_dp - 1:
+                @pl.when(dp < n_dp - 1)
+                def _():
+                    sent(me, 0, step + 1)
+            sent(me, 2, step)
+            arrive(elsewhere + dp - 1 - step, 2, step)
+
+        @pl.when(dp + 1 + step <= n_dp - 1)
+        def _(step=step):
+            if step + 1 < n_dp - 1:
+                @pl.when(dp > 0)
+                def _():
+                    sent(me, 1, step + 1)
+            sent(me, 3, step)
+            arrive(elsewhere + dp + 1 + step, 3, step)
+
+
+def gather_all(features, w_in, w_out, answers):
+    n_dp, n_mp = lax.axis_size("dp"), lax.axis_size("mp")
+    owners = answers.shape[0]
+    items, in_part = features.shape
+    dma = pltpu.SemaphoreType.DMA
+    anywhere = pl.BlockSpec(memory_space=pl.ANY)
+    return pl.pallas_call(
+        gather_kernel,
+        out_shape=(
+            jax.ShapeDtypeStruct((items, n_mp * in_part), BF16),
+            jax.ShapeDtypeStruct((owners, *w_in.shape), BF16),
+            jax.ShapeDtypeStruct((owners, *w_out.shape), BF16),
+            jax.ShapeDtypeStruct(answers.shape, BF16),
+        ),
+        in_specs=[anywhere] * 4,
+        out_specs=[anywhere] * 4,
+        scratch_shapes=[
+            dma((4,)), dma((n_mp + 1,)), dma((n_mp + 1,)),
+            dma((2, n_dp, 2)), dma((2, n_dp, 2)), dma((2, n_dp, 2)), dma((2, n_dp, 2)),
+            dma((owners,)), dma((owners,)),
+        ],
+        compiler_params=pltpu.CompilerParams(collective_id=0, has_side_effects=True),
+    )(features, w_in, w_out, answers)
+
+
 def shards(features, w_in, w_out, codebook, codes, decoder_grad):
     n_sec, n_dp, n_mp = (lax.axis_size(a) for a in ("section", "dp", "mp"))
     sec, dp, mp = (lax.axis_index(a) for a in ("section", "dp", "mp"))
@@ -78,28 +271,6 @@
     slots = owners * capacity
     items_all = items * owners
 
-    w_parts = [(dp, w_in, w_out)]
-    f_parts = [(mp, features)]
-    for step in range(1, n_dp):
-        w_parts.append((source_of(dp, n_dp, step), shift(w_in, "dp", step), shift(w_out, "dp", step)))
-    for step in range(1, n_mp):
-        f_parts.append((source_of(mp, n_mp, step), shift(features, "mp", step)))
-    blocks = [(sec * n_dp + at, a, b) for at, a, b in w_parts]
-    for step in range(1, n_sec):
-        from_sec = source_of(sec, n_sec, step)
-        blocks += [
-            (from_sec * n_dp + at, shift(a, "section", step), shift(b, "section", step))
-            for at, a, b in w_parts
-        ]
-    w_full = jnp.zeros((owners * in_rows, hid), BF16)
-    out_full = jnp.zeros((owners * out_rows, hid), BF16)
-    for at, a, b in blocks:
-        w_full = lax.dynamic_update_slice(w_full, a, (at * in_rows, 0))
-        out_full = lax.dynamic_update_slice(out_full, b, (at * out_rows, 0))
-    f_full = jnp.zeros((items, n_mp * in_part), BF16)
-    for at, a in f_parts:
-        f_full = lax.dynamic_update_slice(f_full, a, (0, at * in_part))
-
     exchange = functools.partial(
         lax.all_to_all, axis_name=("section", "dp"), split_axis=0, concat_axis=0, tiled=True
     )
@@ -115,7 +286,11 @@
     asked = jnp.sum(jnp.where(hit, local[:, :, None, :], 0), axis=3)
     book = codebook.reshape(levels * rows_own, width)
     flat_asked = asked + (jnp.arange(levels) * rows_own)[None, :, None]
-    answers = exchange(jnp.take(book, flat_asked, axis=0, mode="clip"))
+    f_full, w_full, out_full, answers = gather_all(
+        features, w_in, w_out, jnp.take(book, flat_asked, axis=0, mode="clip")
+    )
+    w_full = w_full.reshape(owners * in_rows, hid)
+    out_full = out_full.reshape(owners * out_rows, hid)
     owner_of = codes // rows_own
     same = (owner_of[:, :, None] == owner_of[:, None, :]) & before.T[None]
     ranking = jnp.sum(same.astype(jnp.int32), axis=2)
@@ -181,8 +356,8 @@
     def out_chunk(at):
         return over_items(lax.dynamic_slice(grad_full, (0, at * out_rows), (items, out_rows)), hidden)
 
-    def scattered(chunk):
-        total = None
+    def scattered(chunk, sums):
+        parts = []
         for step in list(range(n_dp - 1, 0, -1)) + [0]:
             goes_to = target_of(dp, n_dp, step) if step else dp
             pair = None
@@ -194,11 +369,16 @@
                 pair = part if pair is None else pair + part
             if step:
                 pair = shift(pair.astype(BF16), "dp", step).astype(F32)
-            total = pair if total is None else total + pair
-        return total
-
-    out_grad = scattered(out_chunk)
-    in_grad = scattered(in_chunk)
+            elif sums is not None:
+                pair, sums = lax.optimization_barrier((pair, sums))
+            parts.append(pair)
+        total = parts[-1]
+        for pair in parts[:-1]:
+            total = total + pair
+        return total, sums
+
+    out_grad, _ = scattered(out_chunk, None)
+    in_grad, code_sums = scattered(in_chunk, code_sums)
     return (in_grad, out_grad, code_sums)
 
 

time: 271 us -> 206 us (0.76)
  the two profiles are of different devices: /device:TPU:8 before, /device:TPU:0 now
where the time goes in v2:
time: 206 us
  Pallas kernels  91.2 us (44%)
  waiting for transfers between devices  37.9 us (18%)
  starting transfers between devices  27.8 us (13%)
  matrix products  21.8 us (11%)
  local copies, waits for them, and re-layouts  20.4 us (10%)
  other arithmetic  5.44 us (3%)
    pallas_call x1, Pallas kernels, gather_all(): pl.pallas_call(gather_kernel, out_shape=(jax.ShapeDtypeStruct((items, n_m...  63.3 us
    ppermute x20, waiting for transfers between devices, shift(): return lax.ppermute(value, axis, partner_pairs(lax.axis_size(axis), step))  33.7 us
    pallas_call x1, Pallas kernels, sum_rows(): pl.pallas_call(sums_kernel, grid=(levels, rows_own // tile), in_specs=[pl...  27.9 us
    ppermute x20, starting transfers between devices, shift(): return lax.ppermute(value, axis, partner_pairs(lax.axis_size(axis), step))  17.7 us
    gather x1, local copies, waits for them, and re-layouts, shards(): jnp.take(book, flat_asked, axis=0, mode='clip')  14.6 us
    dot_general x1, matrix products, shards(): preact = jnp.dot(f_full, w_full, preferred_element_type=F32)  6.88 us
    all_to_all x1, starting transfers between devices, shards(): all_codes = exchange(jnp.broadcast_to(codes[None], (owners, levels, items)))  6.33 us
    dot_general x8, matrix products, in_chunk(): over_items(lax.dynamic_slice(f_full, (0, at * in_rows), (items, in_rows))...  6.21 us
  transfers between devices with their start and end apart: 22, of which 6 were waited for; matrix products, arithmetic and copies ran while one was open for 10% of the time, Pallas kernels for 14%

profile of v2, /device:TPU:0, one launch (start us, length us, event | category | flops | bytes accessed | tf_op | source)
XLA Modules:
  0.0 205.6 jit_solution(8345667460097496734)
XLA Ops:
  0.6 1.3 broadcast_in_dim.25
  2.0 6.3 %all-to-all-start = ((s32[8,3,512]{2,1,0:T(4,128)}), s32[8,3,512]{2,1,0:T(4,128)S(1)}, u32[]{:S(2)}, u32[]{:S(2)}) async-start(s32[8,3,512]{2,1,0:T(4,128)} %broadcast_in_dim.25), calls=%async_computation | async-start | bytes 131072 | tf_op jit(solution)/shard_map/all_to_all | solution.py:277
  8.3 0.7 add_select_fusion.2
  9.1 1.0 convert_reduce_fusion
  10.1 4.2 %all-to-all-done = s32[8,3,512]{2,1,0:T(4,128)S(1)} async-done(((s32[8,3,512]{2,1,0:T(4,128)}), s32[8,3,512]{2,1,0:T(4,128)S(1)}, u32[]{:S(2)}, u32[]{:S(2)}) %all-to-all-start) | async-done | bytes 49184 | tf_op jit(solution)/shard_map/all_to_all | solution.py:277
  14.8 0.7 select_reduce_fusion
  15.6 14.6 %gather_fusion = bf16[3072,128]{1,0:T(8,128)(2,1)} fusion(bf16[24576,128]{1,0:T(8,128)(2,1)} %bitcast.51, s32[3072]{0:T(1024)S(1)} %broadcast_clamp_fusion), kind=kCustom, calls=%fused_computation | custom fusion | bytes 1585152 | tf_op jit(solution)/shard_map/jit(_take)/gather | solution.py:290
  30.2 63.3 %shard_map.85 = (bf16[512,4096]{1,0:T(8,128)(2,1)}, bf16[8,512,512]{2,1,0:T(8,128)(2,1)}, bf16[8,64,512]{2,1,0:T(8,128)(2,1)}, bf16[8,3,128,128]{3,2,1,0:T(8,128)(2,1)}) custom-call(bf16[512,1024]{1,0:T(8,128)(2,1)} %f_ref.1, bf16[512,512]{1,0:T(8,128)(2,1)} %w_ref.1, bf16[64,512]{1,0:T(8,128)(2,1)} %o_ref.1, bf16[8,3,128,128]{3,2,1,0:T(8,128)(2,1)} %bitcast.53), custom_call_target="tpu_custom_call" | custom-call | tf_op jit(solution)/shard_map/pallas_call | solution.py:242
  93.5 6.9 %multiply_convert_fusion = (bf16[512,512]{1,0:T(8,128)(2,1)S(1)}, f32[512,512]{1,0:T(8,128)}) fusion(bf16[512,4096]{1,0:T(8,128)(2,1)} %get-tuple-element.9, bf16[4096,512]{1,0:T(8,128)(2,1)} %bitcast.61), kind=kOutput, calls=%fused_computation.26 | convolution fusion | flops 2148794368 | bytes 9961472 | tf_op jit(solution)/shard_map/dot_general | solution.py:305
  101.3 1.7 collective-permute-start
  103.0 1.6 collective-permute-start.1
  104.9 0.6 multiply_add_fusion
  105.5 3.2 %gather_fusion.1 = bf16[1536,128]{1,0:T(8,128)(2,1)S(1)} fusion(bf16[3072,128]{1,0:T(8,128)(2,1)S(1)} %bitcast.50, s32[2048]{0:T(1024)S(1)} %pad_clamp_fusion), kind=kCustom, calls=%fused_computation.1 | custom fusion | bytes 792576 | tf_op jit(solution)/shard_map/jit(_take)/gather | solution.py:298
  108.7 1.8 collective-permute-done
  110.5 6.5 %collective-permute-done.1 = f32[512,128]{1,0:T(8,128)} collective-permute-done((f32[512,128]{1,0:T(8,128)S(1)}, f32[512,128]{1,0:T(8,128)}, u32[]{:S(2)}, u32[]{:S(2)}) %collective-permute-start.1) | collective-permute-done | bytes 262176 | tf_op jit(solution)/shard_map/ppermute | solution.py:34
  117.1 1.4 constant_dynamic-update-slice_fusion.3
  118.5 1.7 collective-permute-start.4
  120.2 0.4 collective-permute-start.3
  120.6 1.4 collective-permute-start.5
  122.1 1.9 fusion.2
  124.0 0.9 copy.22
  124.9 3.7 %all-to-all-start.1 = ((bf16[8,3,128,128]{3,2,1,0:T(8,128)(2,1)}), bf16[8,3,128,128]{3,2,1,0:T(8,128)(2,1)S(1)}, u32[]{:S(2)}, u32[]{:S(2)}) async-start(bf16[8,3,128,128]{3,2,1,0:T(8,128)(2,1)} %bitcast.47), calls=%async_computation.1 | async-start | bytes 1572864 | tf_op jit(solution)/shard_map/all_to_all | solution.py:338
  128.9 2.0 fusion.3
  130.8 0.3 convolution_convert_fusion.4
  131.2 0.3 convolution_convert_fusion.5
  131.5 0.3 convolution_convert_fusion.6
  131.8 0.3 convolution_convert_fusion.7
  133.2 0.5 convolution_convert_fusion
  133.7 0.5 convolution_convert_fusion.1
  134.2 0.5 convolution_convert_fusion.2
  134.6 0.5 convolution_convert_fusion.3
  135.7 0.3 add_convert_fusion.5
  136.0 3.6 %collective-permute-start.15 = (bf16[64,512]{1,0:T(8,128)(2,1)S(1)}, bf16[64,512]{1,0:T(8,128)(2,1)S(1)}, u32[]{:S(2)}, u32[]{:S(2)}) collective-permute-start(bf16[64,512]{1,0:T(8,128)(2,1)S(1)} %add_convert_fusion.5), channel_id=1, source_target_pairs={{0,12},{4,8},{8,4},{12,0},{1,13},{5,9},{9,5},{13,1},{2,14},{6,10},... | collective-permute-start | bytes 196616 | tf_op jit(solution)/shard_map/ppermute | solution.py:34
  139.6 0.3 add_convert_fusion.4
  140.0 0.3 add_convert_fusion.3
  140.3 0.9 collective-permute-start.19
  141.5 6.6 %collective-permute-done.15 = bf16[64,512]{1,0:T(8,128)(2,1)S(1)} collective-permute-done((bf16[64,512]{1,0:T(8,128)(2,1)S(1)}, bf16[64,512]{1,0:T(8,128)(2,1)S(1)}, u32[]{:S(2)}, u32[]{:S(2)}) %collective-permute-start.15) | collective-permute-done | bytes 65568 | tf_op jit(solution)/shard_map/ppermute | solution.py:34
  148.1 6.9 %collective-permute-done.17 = bf16[64,512]{1,0:T(8,128)(2,1)S(1)} collective-permute-done((bf16[64,512]{1,0:T(8,128)(2,1)S(1)}, bf16[64,512]{1,0:T(8,128)(2,1)S(1)}, u32[]{:S(2)}, u32[]{:S(2)}) %collective-permute-start.17) | collective-permute-done | bytes 65568 | tf_op jit(solution)/shard_map/ppermute | solution.py:34
  155.1 0.7 convert_add_fusion.2
  155.8 1.3 add_convert_fusion.2
  157.0 1.3 collective-permute-start.8
  158.4 1.3 add_convert_fusion.1
  159.9 1.3 add_convert_fusion
  161.2 2.8 %collective-permute-start.12 = (bf16[512,512]{1,0:T(8,128)(2,1)}, bf16[512,512]{1,0:T(8,128)(2,1)S(1)}, u32[]{:S(2)}, u32[]{:S(2)}) collective-permute-start(bf16[512,512]{1,0:T(8,128)(2,1)} %add_convert_fusion), channel_id=1, source_target_pairs={{0,4},{4,0},{8,12},{12,8},{1,5},{5,1},{9,13},{13,9},{2,6},{6,2},{1... | collective-permute-start | bytes 1572872 | tf_op jit(solution)/shard_map/ppermute | solution.py:34
  164.0 0.5 convert_add_fusion.1
  164.6 27.9 %shard_map.86 = f32[3,8192,128]{2,1,0:T(8,128)} custom-call(s32[3,1,1024]{2,1,0:T(1,128)S(1)} %bitcast.49, bf16[3,1024,128]{2,1,0:T(8,128)(2,1)S(1)} %bitcast.48), custom_call_target="tpu_custom_call" | custom-call | flops 6442450944 | bytes 12582912 | tf_op jit(solution)/shard_map/pallas_call | solution.py:50
  192.5 11.9 %collective-permute-done.10 = bf16[512,512]{1,0:T(8,128)(2,1)S(1)} collective-permute-done((bf16[512,512]{1,0:T(8,128)(2,1)}, bf16[512,512]{1,0:T(8,128)(2,1)S(1)}, u32[]{:S(2)}, u32[]{:S(2)}) %collective-permute-start.10) | collective-permute-done | bytes 524320 | tf_op jit(solution)/shard_map/ppermute | solution.py:34
  204.4 1.3 convert_add_fusion
  (60 shorter events, 4.4 us)
Async XLA Ops:
  2.0 12.3 %all-to-all-start = ((s32[8,3,512]{2,1,0:T(4,128)}), s32[8,3,512]{2,1,0:T(4,128)S(1)}, u32[]{:S(2)}, u32[]{:S(2)}) async-start(s32[8,3,512]{2,1,0:T(4,128)} %broadcast_in_dim.25), calls=%async_computation | async-start | bytes 131072 | tf_op jit(solution)/shard_map/all_to_all | solution.py:277
  93.5 6.9 %copy-start.1 = (bf16[8,64,512]{2,1,0:T(8,128)(2,1)S(1)}, bf16[8,64,512]{2,1,0:T(8,128)(2,1)}, u32[]{:S(2)}) copy-start(bf16[8,64,512]{2,1,0:T(8,128)(2,1)} %get-tuple-element.11) | copy-start | bytes 1572868
  93.5 11.4 %copy-start.3 = (s32[3,512]{1,0:T(4,128)S(1)}, s32[3,512]{1,0:T(4,128)}, u32[]{:S(2)}) copy-start(s32[3,512]{1,0:T(4,128)} %param.10) | copy-start | bytes 18436
  100.4 5.1 %copy-start = (bf16[8,3,128,128]{3,2,1,0:T(8,128)(2,1)S(1)}, bf16[8,3,128,128]{3,2,1,0:T(8,128)(2,1)}, u32[]{:S(2)}) copy-start(bf16[8,3,128,128]{3,2,1,0:T(8,128)(2,1)} %get-tuple-element.12) | copy-start | bytes 2359300
  100.4 16.7 %copy-start.2 = (bf16[512,128]{1,0:T(8,128)(2,1)S(1)}, bf16[512,128]{1,0:T(8,128)(2,1)}, u32[]{:S(2)}) copy-start(bf16[512,128]{1,0:T(8,128)(2,1)} %param.11) | copy-start | bytes 393220
  101.3 9.2 %collective-permute-start = (f32[512,128]{1,0:T(8,128)S(1)}, f32[512,128]{1,0:T(8,128)S(1)}, u32[]{:S(2)}, u32[]{:S(2)}) collective-permute-start(f32[512,128]{1,0:T(8,128)S(1)} %fusion.56), channel_id=1, source_target_pairs={{0,1},{1,0},{2,3},{3,2},{4,5},{5,4},{6,7},{7,6},{8,9},{9,8},{10,11... | collective-permute-start | bytes 786440 | tf_op jit(solution)/shard_map/ppermute | solution.py:34
  103.0 14.0 %collective-permute-start.1 = (f32[512,128]{1,0:T(8,128)S(1)}, f32[512,128]{1,0:T(8,128)}, u32[]{:S(2)}, u32[]{:S(2)}) collective-permute-start(f32[512,128]{1,0:T(8,128)S(1)} %fusion.54), channel_id=1, source_target_pairs={{0,2},{1,3},{2,0},{3,1},{4,6},{5,7},{6,4},{7,5},{8,10},{9,11},{10,... | collective-permute-start | bytes 786440 | tf_op jit(solution)/shard_map/ppermute | solution.py:34
  104.7 12.4 %collective-permute-start.2 = (f32[512,128]{1,0:T(8,128)S(1)}, f32[512,128]{1,0:T(8,128)}, u32[]{:S(2)}, u32[]{:S(2)}) collective-permute-start(f32[512,128]{1,0:T(8,128)S(1)} %fusion.52), channel_id=1, source_target_pairs={{0,3},{1,2},{2,1},{3,0},{4,7},{5,6},{6,5},{7,4},{8,11},{9,10},{10,... | collective-permute-start | bytes 786440 | tf_op jit(solution)/shard_map/ppermute | solution.py:34
  118.5 10.2 %collective-permute-start.4 = (bf16[512,128]{1,0:T(8,128)(2,1)S(1)}, bf16[512,128]{1,0:T(8,128)(2,1)S(1)}, u32[]{:S(2)}, u32[]{:S(2)}) collective-permute-start(bf16[512,128]{1,0:T(8,128)(2,1)S(1)} %get-tuple-element.16), channel_id=1, source_target_pairs={{0,2},{1,3},{2,0},{3,1},{4,6},{5,7},{6,4},{7,5},{8,10},{9,11},{10,... | collective-permute-start | bytes 393224 | tf_op jit(solution)/shard_map/ppermute | solution.py:34
  120.2 8.5 %collective-permute-start.3 = (bf16[512,128]{1,0:T(8,128)(2,1)S(1)}, bf16[512,128]{1,0:T(8,128)(2,1)S(1)}, u32[]{:S(2)}, u32[]{:S(2)}) collective-permute-start(bf16[512,128]{1,0:T(8,128)(2,1)S(1)} %get-tuple-element.16), channel_id=1, source_target_pairs={{0,1},{1,0},{2,3},{3,2},{4,5},{5,4},{6,7},{7,6},{8,9},{9,8},{10,11... | collective-permute-start | bytes 393224 | tf_op jit(solution)/shard_map/ppermute | solution.py:34
  120.6 8.2 %collective-permute-start.5 = (bf16[512,128]{1,0:T(8,128)(2,1)S(1)}, bf16[512,128]{1,0:T(8,128)(2,1)S(1)}, u32[]{:S(2)}, u32[]{:S(2)}) collective-permute-start(bf16[512,128]{1,0:T(8,128)(2,1)S(1)} %get-tuple-element.16), channel_id=1, source_target_pairs={{0,3},{1,2},{2,1},{3,0},{4,7},{5,6},{6,5},{7,4},{8,11},{9,10},{10,... | collective-permute-start | bytes 393224 | tf_op jit(solution)/shard_map/ppermute | solution.py:34
  124.9 39.5 %all-to-all-start.1 = ((bf16[8,3,128,128]{3,2,1,0:T(8,128)(2,1)}), bf16[8,3,128,128]{3,2,1,0:T(8,128)(2,1)S(1)}, u32[]{:S(2)}, u32[]{:S(2)}) async-start(bf16[8,3,128,128]{3,2,1,0:T(8,128)(2,1)} %bitcast.47), calls=%async_computation.1 | async-start | bytes 1572864 | tf_op jit(solution)/shard_map/all_to_all | solution.py:338
  128.8 4.3 %copy-start.4 = (bf16[512,4096]{1,0:T(8,128)(2,1)S(1)}, bf16[512,4096]{1,0:T(8,128)(2,1)}, u32[]{:S(2)}) copy-start(bf16[512,4096]{1,0:T(8,128)(2,1)} %get-tuple-element.9) | copy-start | bytes 12582916
  132.1 8.2 %collective-permute-start.13 = (bf16[64,512]{1,0:T(8,128)(2,1)S(1)}, bf16[64,512]{1,0:T(8,128)(2,1)S(1)}, u32[]{:S(2)}, u32[]{:S(2)}) collective-permute-start(bf16[64,512]{1,0:T(8,128)(2,1)S(1)} %convolution_convert_fusion.7), channel_id=1, source_target_pairs={{0,16},{16,0},{1,17},{17,1},{2,18},{18,2},{3,19},{19,3},{4,20},{20... | collective-permute-start | bytes 196616 | tf_op jit(solution)/shard_map/ppermute | solution.py:34
  132.4 3.0 %collective-permute-start.14 = (bf16[64,512]{1,0:T(8,128)(2,1)S(1)}, bf16[64,512]{1,0:T(8,128)(2,1)S(1)}, u32[]{:S(2)}, u32[]{:S(2)}) collective-permute-start(bf16[64,512]{1,0:T(8,128)(2,1)S(1)} %convolution_convert_fusion.6), channel_id=1, source_target_pairs={{0,16},{16,0},{1,17},{17,1},{2,18},{18,2},{3,19},{19,3},{4,20},{20... | collective-permute-start | bytes 196616 | tf_op jit(solution)/shard_map/ppermute | solution.py:34
  132.7 3.3 %collective-permute-start.16 = (bf16[64,512]{1,0:T(8,128)(2,1)S(1)}, bf16[64,512]{1,0:T(8,128)(2,1)S(1)}, u32[]{:S(2)}, u32[]{:S(2)}) collective-permute-start(bf16[64,512]{1,0:T(8,128)(2,1)S(1)} %convolution_convert_fusion.5), channel_id=1, source_target_pairs={{0,16},{16,0},{1,17},{17,1},{2,18},{18,2},{3,19},{19,3},{4,20},{20... | collective-permute-start | bytes 196616 | tf_op jit(solution)/shard_map/ppermute | solution.py:34
  132.9 7.0 %collective-permute-start.18 = (bf16[64,512]{1,0:T(8,128)(2,1)S(1)}, bf16[64,512]{1,0:T(8,128)(2,1)S(1)}, u32[]{:S(2)}, u32[]{:S(2)}) collective-permute-start(bf16[64,512]{1,0:T(8,128)(2,1)S(1)} %convolution_convert_fusion.4), channel_id=1, source_target_pairs={{0,16},{16,0},{1,17},{17,1},{2,18},{18,2},{3,19},{19,3},{4,20},{20... | collective-permute-start | bytes 196616 | tf_op jit(solution)/shard_map/ppermute | solution.py:34
  135.1 20.6 %collective-permute-start.7 = (bf16[512,512]{1,0:T(8,128)(2,1)S(1)}, bf16[512,512]{1,0:T(8,128)(2,1)S(1)}, u32[]{:S(2)}, u32[]{:S(2)}) collective-permute-start(bf16[512,512]{1,0:T(8,128)(2,1)S(1)} %convolution_convert_fusion.2), channel_id=1, source_target_pairs={{0,16},{16,0},{1,17},{17,1},{2,18},{18,2},{3,19},{19,3},{4,20},{20... | collective-permute-start | bytes 1572872 | tf_op jit(solution)/shard_map/ppermute | solution.py:34
  135.4 23.0 %collective-permute-start.9 = (bf16[512,512]{1,0:T(8,128)(2,1)S(1)}, bf16[512,512]{1,0:T(8,128)(2,1)S(1)}, u32[]{:S(2)}, u32[]{:S(2)}) collective-permute-start(bf16[512,512]{1,0:T(8,128)(2,1)S(1)} %convolution_convert_fusion.1), channel_id=1, source_target_pairs={{0,16},{16,0},{1,17},{17,1},{2,18},{18,2},{3,19},{19,3},{4,20},{20... | collective-permute-start | bytes 1572872 | tf_op jit(solution)/shard_map/ppermute | solution.py:34
  136.0 12.1 %collective-permute-start.15 = (bf16[64,512]{1,0:T(8,128)(2,1)S(1)}, bf16[64,512]{1,0:T(8,128)(2,1)S(1)}, u32[]{:S(2)}, u32[]{:S(2)}) collective-permute-start(bf16[64,512]{1,0:T(8,128)(2,1)S(1)} %add_convert_fusion.5), channel_id=1, source_target_pairs={{0,12},{4,8},{8,4},{12,0},{1,13},{5,9},{9,5},{13,1},{2,14},{6,10},... | collective-permute-start | bytes 196616 | tf_op jit(solution)/shard_map/ppermute | solution.py:34
  139.9 15.1 %collective-permute-start.17 = (bf16[64,512]{1,0:T(8,128)(2,1)S(1)}, bf16[64,512]{1,0:T(8,128)(2,1)S(1)}, u32[]{:S(2)}, u32[]{:S(2)}) collective-permute-start(bf16[64,512]{1,0:T(8,128)(2,1)S(1)} %add_convert_fusion.4), channel_id=1, source_target_pairs={{0,8},{4,12},{8,0},{12,4},{1,9},{5,13},{9,1},{13,5},{2,10},{6,14},... | collective-permute-start | bytes 196616 | tf_op jit(solution)/shard_map/ppermute | solution.py:34
  140.3 14.7 %collective-permute-start.19 = (bf16[64,512]{1,0:T(8,128)(2,1)S(1)}, bf16[64,512]{1,0:T(8,128)(2,1)S(1)}, u32[]{:S(2)}, u32[]{:S(2)}) collective-permute-start(bf16[64,512]{1,0:T(8,128)(2,1)S(1)} %add_convert_fusion.3), channel_id=1, source_target_pairs={{0,4},{4,0},{8,12},{12,8},{1,5},{5,1},{9,13},{13,9},{2,6},{6,2},{1... | collective-permute-start | bytes 196616 | tf_op jit(solution)/shard_map/ppermute | solution.py:34
  148.1 15.9 %collective-permute-start.6 = (bf16[512,512]{1,0:T(8,128)(2,1)S(1)}, bf16[512,512]{1,0:T(8,128)(2,1)S(1)}, u32[]{:S(2)}, u32[]{:S(2)}) collective-permute-start(bf16[512,512]{1,0:T(8,128)(2,1)S(1)} %convolution_convert_fusion.3), channel_id=1, source_target_pairs={{0,16},{16,0},{1,17},{17,1},{2,18},{18,2},{3,19},{19,3},{4,20},{20... | collective-permute-start | bytes 1572872 | tf_op jit(solution)/shard_map/ppermute | solution.py:34
  155.1 4.9 %collective-permute-start.11 = (bf16[512,512]{1,0:T(8,128)(2,1)S(1)}, bf16[512,512]{1,0:T(8,128)(2,1)S(1)}, u32[]{:S(2)}, u32[]{:S(2)}) collective-permute-start(bf16[512,512]{1,0:T(8,128)(2,1)S(1)} %convolution_convert_fusion), channel_id=1, source_target_pairs={{0,16},{16,0},{1,17},{17,1},{2,18},{18,2},{3,19},{19,3},{4,20},{20... | collective-permute-start | bytes 1572872 | tf_op jit(solution)/shard_map/ppermute | solution.py:34
  157.0 35.5 %collective-permute-start.8 = (bf16[512,512]{1,0:T(8,128)(2,1)}, bf16[512,512]{1,0:T(8,128)(2,1)S(1)}, u32[]{:S(2)}, u32[]{:S(2)}) collective-permute-start(bf16[512,512]{1,0:T(8,128)(2,1)} %add_convert_fusion.2), channel_id=1, source_target_pairs={{0,12},{4,8},{8,4},{12,0},{1,13},{5,9},{9,5},{13,1},{2,14},{6,10},... | collective-permute-start | bytes 1572872 | tf_op jit(solution)/shard_map/ppermute | solution.py:34
  159.7 44.7 %collective-permute-start.10 = (bf16[512,512]{1,0:T(8,128)(2,1)}, bf16[512,512]{1,0:T(8,128)(2,1)S(1)}, u32[]{:S(2)}, u32[]{:S(2)}) collective-permute-start(bf16[512,512]{1,0:T(8,128)(2,1)} %add_convert_fusion.1), channel_id=1, source_target_pairs={{0,8},{4,12},{8,0},{12,4},{1,9},{5,13},{9,1},{13,5},{2,10},{6,14},... | collective-permute-start | bytes 1572872 | tf_op jit(solution)/shard_map/ppermute | solution.py:34
  161.2 43.2 %collective-permute-start.12 = (bf16[512,512]{1,0:T(8,128)(2,1)}, bf16[512,512]{1,0:T(8,128)(2,1)S(1)}, u32[]{:S(2)}, u32[]{:S(2)}) collective-permute-start(bf16[512,512]{1,0:T(8,128)(2,1)} %add_convert_fusion), channel_id=1, source_target_pairs={{0,4},{4,0},{8,12},{12,8},{1,5},{5,1},{9,13},{13,9},{2,6},{6,2},{1... | collective-permute-start | bytes 1572872 | tf_op jit(solution)/shard_map/ppermute | solution.py:34

commit v3 on v2

--- a/solution.py
+++ b/solution.py
@@ -66,8 +66,8 @@
 
 
 def gather_kernel(
-    f_ref, w_ref, o_ref, ans_ref, f_out, w_out, o_out, ans_out,
-    local_sem, f_send, f_recv, dp_send, dp_recv, sec_send, sec_recv, ans_send, ans_recv,
+    f_ref, fx_ref, fy_ref, w_ref, r1_ref, r2_ref, l1_ref, l2_ref, o_ref, ans_ref,
+    f_out, w_out, o_out, ans_out, local_sem, early_sem, f_send, f_recv, dp_send, dp_recv, sec_send, sec_recv, ans_send, ans_recv,
 ):
     n_dp, n_mp = lax.axis_size("dp"), lax.axis_size("mp")
     sec, dp, mp = (lax.axis_index(a) for a in ("section", "dp", "mp"))
@@ -105,26 +105,37 @@
         answers.append(remote(ans_ref.at[at], ans_out.at[me], ans_send.at[step], ans_recv.at[step], to))
         answers[-1].start()
 
-    relay = n_mp == 4
-    feature = [
-        remote(
-            f_ref, f_out.at[:, columns(mp)], f_send.at[step], f_recv.at[step],
-            {"mp": target_of(mp, n_mp, step)},
+    half = items // 2
+    early = ((r1_ref, r2_ref), (l1_ref, l2_ref))
+    halves = []
+    for k, (ref, to) in enumerate(((fx_ref, mp ^ 2), (fy_ref, mp ^ 1))):
+        rows = pl.ds(k * half, half)
+        halves.append(
+            remote(
+                ref.at[rows], f_out.at[rows, columns(to ^ 3)], f_send.at[k], f_recv.at[k], {"mp": to}
+            )
         )
-        for step in (range(1, 3) if relay else range(1, n_mp))
-    ]
 
     def weights(block, src, side, step, to):
-        sems = (dp_send, dp_recv) if side < 2 else (sec_send, sec_recv)
-        place = side if side < 2 else side - 2
-        pairs = ((w_ref, w_out), (o_ref, o_out))
-        return [
-            remote(
-                own if src is None else out.at[src], out.at[block],
-                sems[0].at[place, step, k], sems[1].at[place, step, k], to,
+        along = side < 2
+        place = side if along else side - 2
+        sems = (dp_send, dp_recv) if along else (sec_send, sec_recv)
+        came = step - 1 if along else step
+        copies = []
+        for k, (own, out) in enumerate(((w_ref, w_out), (o_ref, o_out))):
+            if k == 0 and along and step < 2:
+                continue
+            held = early[place][came] if k == 0 and 0 <= came < 2 else out.at[block]
+            copies.append(
+                remote(
+                    own if src is None else held, out.at[block],
+                    sems[0].at[place, step, k], sems[1].at[place, step, k], to,
+                )
             )
-            for k, (own, out) in enumerate(pairs)
-        ]
+        return copies
+
+    def early_copy(block, side, step):
+        return pltpu.make_async_copy(early[side][step], w_out.at[block], early_sem.at[side, step])
 
     def start(copies):
         for copy in copies:
@@ -140,11 +151,13 @@
     def _():
         start(weights(me, None, 1, 0, left))
 
-    start(feature)
+    start(halves)
     own_sec = weights(me, None, 2, n_dp - 1, other)
     start(own_sec)
     locals_ = [
         pltpu.make_async_copy(f_ref, f_out.at[:, columns(mp)], local_sem.at[0]),
+        pltpu.make_async_copy(fx_ref, f_out.at[:, columns(mp ^ 1)], local_sem.at[4]),
+        pltpu.make_async_copy(fy_ref, f_out.at[:, columns(mp ^ 2)], local_sem.at[5]),
         pltpu.make_async_copy(w_ref, w_out.at[me], local_sem.at[1]),
         pltpu.make_async_copy(o_ref, o_out.at[me], local_sem.at[2]),
         pltpu.make_async_copy(ans_ref.at[me], ans_out.at[me], local_sem.at[3]),
@@ -155,11 +168,12 @@
         for copy in weights(block, block, side, step, other):
             copy.wait_recv()
 
-    halves = []
     for step in range(n_dp - 1):
         @pl.when(dp - 1 - step >= 0)
         def _(step=step):
             block = base + dp - 1 - step
+            if step < 2:
+                early_copy(block, 0, step).start()
             arrive(block, 0, step)
             if step + 1 < n_dp - 1:
                 @pl.when(dp < n_dp - 1)
@@ -170,6 +184,8 @@
         @pl.when(dp + 1 + step <= n_dp - 1)
         def _(step=step):
             block = base + dp + 1 + step
+            if step < 2:
+                early_copy(block, 1, step).start()
             arrive(block, 1, step)
             if step + 1 < n_dp - 1:
                 @pl.when(dp > 0)
@@ -177,25 +193,13 @@
                     start(weights(block, block, 1, step + 1, left))
             start(weights(block, block, 3, step, other))
 
-        if step == 0:
-            for copy in feature:
-                copy.wait_recv()
-            if relay:
-                half = items // 2
-                for k, (source, to) in enumerate(((mp ^ 1, mp ^ 2), (mp ^ 2, mp ^ 1))):
-                    view = f_out.at[pl.ds(k * half, half), columns(source)]
-                    halves.append(remote(view, view, f_send.at[3 + k], f_recv.at[3 + k], {"mp": to}))
-                start(halves)
-
     for copy in locals_ + answers:
         copy.wait()
-    for copy in feature:
+    for copy in halves:
         copy.wait_send()
-    if relay:
-        for k in range(2):
-            view = f_out.at[pl.ds(k * (items // 2), items // 2), columns(mp ^ 3)]
-            remote(view, view, f_send.at[3 + k], f_recv.at[3 + k], {"mp": mp ^ 1}).wait_recv()
-            halves[k].wait_send()
+    for k in range(2):
+        view = f_out.at[pl.ds(k * half, half), columns(mp ^ 3)]
+        remote(view, view, f_send.at[k], f_recv.at[k], {"mp": mp ^ 1}).wait_recv()
     elsewhere = (1 - sec) * n_dp
     for copy in own_sec:
         copy.wait_send()
@@ -220,6 +224,8 @@
                 @pl.when(dp < n_dp - 1)
                 def _():
                     sent(me, 0, step + 1)
+            if step < 2:
+                early_copy(base + dp - 1 - step, 0, step).wait()
             sent(me, 2, step)
             arrive(elsewhere + dp - 1 - step, 2, step)
 
@@ -229,11 +235,13 @@
                 @pl.when(dp > 0)
                 def _():
                     sent(me, 1, step + 1)
+            if step < 2:
+                early_copy(base + dp + 1 + step, 1, step).wait()
             sent(me, 3, step)
             arrive(elsewhere + dp + 1 + step, 3, step)
 
 
-def gather_all(features, w_in, w_out, answers):
+def gather_all(features, near, w_in, early, w_out, answers):
     n_dp, n_mp = lax.axis_size("dp"), lax.axis_size("mp")
     owners = answers.shape[0]
     items, in_part = features.shape
@@ -247,15 +255,15 @@
             jax.ShapeDtypeStruct((owners, *w_out.shape), BF16),
             jax.ShapeDtypeStruct(answers.shape, BF16),
         ),
-        in_specs=[anywhere] * 4,
+        in_specs=[anywhere] * 10,
         out_specs=[anywhere] * 4,
         scratch_shapes=[
-            dma((4,)), dma((n_mp + 1,)), dma((n_mp + 1,)),
+            dma((6,)), dma((2, 2)), dma((2,)), dma((2,)),
             dma((2, n_dp, 2)), dma((2, n_dp, 2)), dma((2, n_dp, 2)), dma((2, n_dp, 2)),
             dma((owners,)), dma((owners,)),
         ],
         compiler_params=pltpu.CompilerParams(collective_id=0, has_side_effects=True),
-    )(features, w_in, w_out, answers)
+    )(features, *near, w_in, *early, w_out, answers)
 
 
 def shards(features, w_in, w_out, codebook, codes, decoder_grad):
@@ -271,6 +279,12 @@
     slots = owners * capacity
     items_all = items * owners
 
+    rightward = [(k, k + 1) for k in range(n_dp - 1)]
+    leftward = [(k + 1, k) for k in range(n_dp - 1)]
+    near = (shift(features, "mp", 1), shift(features, "mp", 2))
+    right_1 = lax.ppermute(w_in, "dp", rightward)
+    left_1 = lax.ppermute(w_in, "dp", leftward)
+
     exchange = functools.partial(
         lax.all_to_all, axis_name=("section", "dp"), split_axis=0, concat_axis=0, tiled=True
     )
@@ -286,8 +300,16 @@
     asked = jnp.sum(jnp.where(hit, local[:, :, None, :], 0), axis=3)
     book = codebook.reshape(levels * rows_own, width)
     flat_asked = asked + (jnp.arange(levels) * rows_own)[None, :, None]
+    flat_asked, right_1, left_1 = lax.optimization_barrier((flat_asked, right_1, left_1))
+    right_2 = lax.ppermute(right_1, "dp", rightward)
+    left_2 = lax.ppermute(left_1, "dp", leftward)
     f_full, w_full, out_full, answers = gather_all(
-        features, w_in, w_out, jnp.take(book, flat_asked, axis=0, mode="clip")
+        features,
+        near,
+        w_in,
+        (right_1, right_2, left_1, left_2),
+        w_out,
+        jnp.take(book, flat_asked, axis=0, mode="clip"),
     )
     w_full = w_full.reshape(owners * in_rows, hid)
     out_full = out_full.reshape(owners * out_rows, hid)
@@ -377,8 +399,10 @@
             total = total + pair
         return total, sums
 
-    out_grad, _ = scattered(out_chunk, None)
-    in_grad, code_sums = scattered(in_chunk, code_sums)
+    grads, code_sums = scattered(
+        lambda at: jnp.concatenate([in_chunk(at), out_chunk(at)], axis=0), code_sums
+    )
+    in_grad, out_grad = grads[:in_rows], grads[in_rows:]
     return (in_grad, out_grad, code_sums)
 
 

time: 206 us -> 322 us (1.56)
  the two profiles are of different devices: /device:TPU:0 before, /device:TPU:8 now
where the time goes in v3:
time: 322 us; the launch traced here: 321 us
  Pallas kernels  196 us (61%)
  starting transfers between devices  36.9 us (11%)
  waiting for transfers between devices  36.6 us (11%)
  local copies, waits for them, and re-layouts  23.4 us (7%)
  matrix products  18.7 us (6%)
  other arithmetic  8.08 us (3%)
    pallas_call x1, Pallas kernels, gather_all(): pl.pallas_call(gather_kernel, out_shape=(jax.ShapeDtypeStruct((items, n_m...  168 us
    ppermute x15, waiting for transfers between devices, shift(): return lax.ppermute(value, axis, partner_pairs(lax.axis_size(axis), step))  31.6 us
    pallas_call x1, Pallas kernels, sum_rows(): pl.pallas_call(sums_kernel, grid=(levels, rows_own // tile), in_specs=[pl...  27.9 us
    ppermute x15, starting transfers between devices, shift(): return lax.ppermute(value, axis, partner_pairs(lax.axis_size(axis), step))  15 us
    gather x1, local copies, waits for them, and re-layouts, shards(): jnp.take(book, flat_asked, axis=0, mode='clip')  14.6 us
    dot_general x1, matrix products, shards(): preact = jnp.dot(f_full, w_full, preferred_element_type=F32)  6.87 us
  transfers between devices with their start and end apart: 21, of which 7 were waited for; matrix products, arithmetic and copies ran while one was open for 11% of the time, Pallas kernels for 9%

profile of v3, /device:TPU:8, one launch (start us, length us, event | category | flops | bytes accessed | tf_op | source)
XLA Modules:
  0.0 321.0 jit_solution(14286969113749194501)
XLA Ops:
  0.6 3.5 %collective-permute-start.2 = (bf16[512,512]{1,0:T(8,128)(2,1)}, bf16[512,512]{1,0:T(8,128)(2,1)S(1)}, u32[]{:S(2)}, u32[]{:S(2)}) collective-permute-start(bf16[512,512]{1,0:T(8,128)(2,1)} %w_ref.1), channel_id=1, source_target_pairs={{0,4},{4,8},{8,12},{1,5},{5,9},{9,13},{2,6},{6,10},{10,14},{3,7},{... | collective-permute-start | bytes 1572872 | tf_op jit(solution)/shard_map/ppermute | solution.py:285
  4.1 2.4 collective-permute-start.3
  6.5 1.6 collective-permute-start
  8.1 1.5 collective-permute-start.1
  9.6 1.3 broadcast_in_dim.27
  10.9 5.3 %all-to-all-start = ((s32[8,3,512]{2,1,0:T(4,128)}), s32[8,3,512]{2,1,0:T(4,128)S(1)}, u32[]{:S(2)}, u32[]{:S(2)}) async-start(s32[8,3,512]{2,1,0:T(4,128)} %broadcast_in_dim.27), calls=%async_computation | async-start | bytes 131072 | tf_op jit(solution)/shard_map/all_to_all | solution.py:291
  16.3 0.7 add_select_fusion.2
  17.0 4.4 %all-to-all-done = s32[8,3,512]{2,1,0:T(4,128)S(1)} async-done(((s32[8,3,512]{2,1,0:T(4,128)}), s32[8,3,512]{2,1,0:T(4,128)S(1)}, u32[]{:S(2)}, u32[]{:S(2)}) %all-to-all-start) | async-done | bytes 49184 | tf_op jit(solution)/shard_map/all_to_all | solution.py:291
  21.9 0.7 select_reduce_fusion
  22.7 2.3 collective-permute-start.4
  25.0 4.3 %collective-permute-start.5 = (bf16[512,512]{1,0:T(8,128)(2,1)S(1)}, bf16[512,512]{1,0:T(8,128)(2,1)}, u32[]{:S(2)}, u32[]{:S(2)}) collective-permute-start(bf16[512,512]{1,0:T(8,128)(2,1)S(1)} %collective-permute-done.3.l1_ref), channel_id=1, source_target_pairs={{4,0},{8,4},{12,8},{5,1},{9,5},{13,9},{6,2},{10,6},{14,10},{7,3},{... | collective-permute-start | bytes 1572872 | tf_op jit(solution)/shard_map/ppermute | solution.py:305
  29.4 1.0 convert_reduce_fusion
  30.5 14.6 %gather_fusion = bf16[3072,128]{1,0:T(8,128)(2,1)} fusion(bf16[24576,128]{1,0:T(8,128)(2,1)} %bitcast.47, s32[3072]{0:T(1024)S(1)} %broadcast_clamp_fusion), kind=kCustom, calls=%fused_computation | custom fusion | bytes 1585152 | tf_op jit(solution)/shard_map/jit(_take)/gather | solution.py:312
  45.1 0.9 copy-done.2
  46.4 168.2 %shard_map.85 = (bf16[512,4096]{1,0:T(8,128)(2,1)}, bf16[8,512,512]{2,1,0:T(8,128)(2,1)}, bf16[8,64,512]{2,1,0:T(8,128)(2,1)}, bf16[8,3,128,128]{3,2,1,0:T(8,128)(2,1)}) custom-call(bf16[512,1024]{1,0:T(8,128)(2,1)} %f_ref.1, bf16[512,1024]{1,0:T(8,128)(2,1)} %copy-done.2, bf16[512,1024]{1,0:T(8,128)(2,1)} %copy-done.3, bf16[512,512]{1,0:T(8,128)(2,1)} %w_ref.1, ...), custom_call_target="tpu_custom_call" | custom-call | tf_op jit(solution)/shard_map/pallas_call | solution.py:250
  214.6 6.9 %multiply_convert_fusion = (bf16[512,512]{1,0:T(8,128)(2,1)S(1)}, f32[512,512]{1,0:T(8,128)}) fusion(bf16[512,4096]{1,0:T(8,128)(2,1)} %get-tuple-element.15, bf16[4096,512]{1,0:T(8,128)(2,1)} %bitcast.57), kind=kOutput, calls=%fused_computation.29 | convolution fusion | flops 2148794368 | bytes 9961472 | tf_op jit(solution)/shard_map/dot_general | solution.py:327
  222.4 0.6 collective-permute-start.6
  223.0 0.5 collective-permute-start.7
  223.6 2.4 collective-permute-start.8
  226.1 3.2 gather_fusion.1
  229.3 2.4 collective-permute-done.6
  231.7 4.2 %collective-permute-done.7 = f32[512,128]{1,0:T(8,128)} collective-permute-done((f32[512,128]{1,0:T(8,128)S(1)}, f32[512,128]{1,0:T(8,128)}, u32[]{:S(2)}, u32[]{:S(2)}) %collective-permute-start.7) | collective-permute-done | bytes 262176 | tf_op jit(solution)/shard_map/ppermute | solution.py:34
  236.0 1.4 constant_dynamic-update-slice_fusion.3
  237.4 1.3 collective-permute-start.10
  238.7 0.8 collective-permute-start.9
  239.5 1.4 collective-permute-start.11
  241.0 1.2 fusion.2
  242.2 0.9 copy.22
  243.2 4.1 %all-to-all-start.1 = ((bf16[8,3,128,128]{3,2,1,0:T(8,128)(2,1)}), bf16[8,3,128,128]{3,2,1,0:T(8,128)(2,1)S(1)}, u32[]{:S(2)}, u32[]{:S(2)}) async-start(bf16[8,3,128,128]{3,2,1,0:T(8,128)(2,1)} %bitcast.43), calls=%async_computation.1 | async-start | bytes 1572864 | tf_op jit(solution)/shard_map/all_to_all | solution.py:360
  247.4 2.0 fusion.3
  251.0 0.5 convolution_convert_fusion
  251.5 0.5 convolution_convert_fusion.1
  252.0 0.5 convolution_convert_fusion.2
  252.5 0.5 convolution_convert_fusion.3
  254.9 0.5 fusion.10
  255.8 0.5 fusion.16
  257.6 1.0 fusion.6
  258.8 1.0 fusion.5
  259.8 2.8 collective-permute-start.16
  262.6 1.0 fusion.4
  263.6 0.6 collective-permute-start.14
  264.3 0.5 all-to-all-done.1
  264.9 27.9 %shard_map.86 = f32[3,8192,128]{2,1,0:T(8,128)} custom-call(s32[3,1,1024]{2,1,0:T(1,128)S(1)} %bitcast.45, bf16[3,1024,128]{2,1,0:T(8,128)(2,1)S(1)} %bitcast.44), custom_call_target="tpu_custom_call" | custom-call | flops 6442450944 | bytes 12582912 | tf_op jit(solution)/shard_map/pallas_call | solution.py:50
  292.9 9.9 %collective-permute-done.16 = bf16[576,512]{1,0:T(8,128)(2,1)} collective-permute-done((bf16[576,512]{1,0:T(8,128)(2,1)}, bf16[576,512]{1,0:T(8,128)(2,1)}, u32[]{:S(2)}, u32[]{:S(2)}) %collective-permute-start.16) | collective-permute-done | bytes 589856 | tf_op jit(solution)/shard_map/ppermute | solution.py:34
  302.8 14.7 %collective-permute-done.14 = bf16[576,512]{1,0:T(8,128)(2,1)} collective-permute-done((bf16[576,512]{1,0:T(8,128)(2,1)}, bf16[576,512]{1,0:T(8,128)(2,1)}, u32[]{:S(2)}, u32[]{:S(2)}) %collective-permute-start.14) | collective-permute-done | bytes 589856 | tf_op jit(solution)/shard_map/ppermute | solution.py:34
  317.5 1.8 convert_add_fusion
  319.3 0.7 slice.31
  320.0 1.0 slice.30
  (75 shorter events, 7.8 us)
Async XLA Ops:
  0.6 22.1 %collective-permute-start.2 = (bf16[512,512]{1,0:T(8,128)(2,1)}, bf16[512,512]{1,0:T(8,128)(2,1)S(1)}, u32[]{:S(2)}, u32[]{:S(2)}) collective-permute-start(bf16[512,512]{1,0:T(8,128)(2,1)} %w_ref.1), channel_id=1, source_target_pairs={{0,4},{4,8},{8,12},{1,5},{5,9},{9,13},{2,6},{6,10},{10,14},{3,7},{... | collective-permute-start | bytes 1572872 | tf_op jit(solution)/shard_map/ppermute | solution.py:285
  4.1 18.6 %collective-permute-start.3 = (bf16[512,512]{1,0:T(8,128)(2,1)}, bf16[512,512]{1,0:T(8,128)(2,1)S(1)}, u32[]{:S(2)}, u32[]{:S(2)}) collective-permute-start(bf16[512,512]{1,0:T(8,128)(2,1)} %w_ref.1), channel_id=1, source_target_pairs={{4,0},{8,4},{12,8},{5,1},{9,5},{13,9},{6,2},{10,6},{14,10},{7,3},{... | collective-permute-start | bytes 1572872 | tf_op jit(solution)/shard_map/ppermute | solution.py:286
  6.5 38.6 %collective-permute-start = (bf16[512,1024]{1,0:T(8,128)(2,1)}, bf16[512,1024]{1,0:T(8,128)(2,1)S(1)}, u32[]{:S(2)}, u32[]{:S(2)}) collective-permute-start(bf16[512,1024]{1,0:T(8,128)(2,1)} %f_ref.1), channel_id=1, source_target_pairs={{0,1},{1,0},{2,3},{3,2},{4,5},{5,4},{6,7},{7,6},{8,9},{9,8},{10,11... | collective-permute-start | bytes 3145736 | tf_op jit(solution)/shard_map/ppermute | solution.py:34
  8.1 37.0 %collective-permute-start.1 = (bf16[512,1024]{1,0:T(8,128)(2,1)}, bf16[512,1024]{1,0:T(8,128)(2,1)S(1)}, u32[]{:S(2)}, u32[]{:S(2)}) collective-permute-start(bf16[512,1024]{1,0:T(8,128)(2,1)} %f_ref.1), channel_id=1, source_target_pairs={{0,2},{1,3},{2,0},{3,1},{4,6},{5,7},{6,4},{7,5},{8,10},{9,11},{10,... | collective-permute-start | bytes 3145736 | tf_op jit(solution)/shard_map/ppermute | solution.py:34
  10.9 10.5 %all-to-all-start = ((s32[8,3,512]{2,1,0:T(4,128)}), s32[8,3,512]{2,1,0:T(4,128)S(1)}, u32[]{:S(2)}, u32[]{:S(2)}) async-start(s32[8,3,512]{2,1,0:T(4,128)} %broadcast_in_dim.27), calls=%async_computation | async-start | bytes 131072 | tf_op jit(solution)/shard_map/all_to_all | solution.py:291
  22.7 22.4 %copy-start.4 = (bf16[512,512]{1,0:T(8,128)(2,1)}, bf16[512,512]{1,0:T(8,128)(2,1)S(1)}, u32[]{:S(2)}) copy-start(bf16[512,512]{1,0:T(8,128)(2,1)S(1)} %collective-permute-done.2.r1_ref) | copy-start | bytes 1572868
  22.7 22.4 %copy-start.5 = (bf16[512,512]{1,0:T(8,128)(2,1)}, bf16[512,512]{1,0:T(8,128)(2,1)S(1)}, u32[]{:S(2)}) copy-start(bf16[512,512]{1,0:T(8,128)(2,1)S(1)} %collective-permute-done.3.l1_ref) | copy-start | bytes 1572868
  22.7 22.4 %collective-permute-start.4 = (bf16[512,512]{1,0:T(8,128)(2,1)S(1)}, bf16[512,512]{1,0:T(8,128)(2,1)}, u32[]{:S(2)}, u32[]{:S(2)}) collective-permute-start(bf16[512,512]{1,0:T(8,128)(2,1)S(1)} %collective-permute-done.2.r1_ref), channel_id=1, source_target_pairs={{0,4},{4,8},{8,12},{1,5},{5,9},{9,13},{2,6},{6,10},{10,14},{3,7},{... | collective-permute-start | bytes 1572872 | tf_op jit(solution)/shard_map/ppermute | solution.py:304
  25.0 20.1 %collective-permute-start.5 = (bf16[512,512]{1,0:T(8,128)(2,1)S(1)}, bf16[512,512]{1,0:T(8,128)(2,1)}, u32[]{:S(2)}, u32[]{:S(2)}) collective-permute-start(bf16[512,512]{1,0:T(8,128)(2,1)S(1)} %collective-permute-done.3.l1_ref), channel_id=1, source_target_pairs={{4,0},{8,4},{12,8},{5,1},{9,5},{13,9},{6,2},{10,6},{14,10},{7,3},{... | collective-permute-start | bytes 1572872 | tf_op jit(solution)/shard_map/ppermute | solution.py:305
  45.1 1.0 copy-start.2
  45.1 1.3 copy-start.3
  214.6 6.9 %copy-start.6 = (bf16[8,64,512]{2,1,0:T(8,128)(2,1)S(1)}, bf16[8,64,512]{2,1,0:T(8,128)(2,1)}, u32[]{:S(2)}) copy-start(bf16[8,64,512]{2,1,0:T(8,128)(2,1)} %get-tuple-element.17) | copy-start | bytes 1572868
  221.5 4.5 %copy-start.8 = (s32[3,512]{1,0:T(4,128)S(1)}, s32[3,512]{1,0:T(4,128)}, u32[]{:S(2)}) copy-start(s32[3,512]{1,0:T(4,128)} %param.10) | copy-start | bytes 18436
  221.5 4.6 %copy-start = (bf16[8,3,128,128]{3,2,1,0:T(8,128)(2,1)S(1)}, bf16[8,3,128,128]{3,2,1,0:T(8,128)(2,1)}, u32[]{:S(2)}) copy-start(bf16[8,3,128,128]{3,2,1,0:T(8,128)(2,1)} %get-tuple-element.18) | copy-start | bytes 2359300
  222.4 9.3 %collective-permute-start.6 = (f32[512,128]{1,0:T(8,128)S(1)}, f32[512,128]{1,0:T(8,128)S(1)}, u32[]{:S(2)}, u32[]{:S(2)}) collective-permute-start(f32[512,128]{1,0:T(8,128)S(1)} %fusion.51), channel_id=1, source_target_pairs={{0,1},{1,0},{2,3},{3,2},{4,5},{5,4},{6,7},{7,6},{8,9},{9,8},{10,11... | collective-permute-start | bytes 786440 | tf_op jit(solution)/shard_map/ppermute | solution.py:34
  223.0 12.9 %collective-permute-start.7 = (f32[512,128]{1,0:T(8,128)S(1)}, f32[512,128]{1,0:T(8,128)}, u32[]{:S(2)}, u32[]{:S(2)}) collective-permute-start(f32[512,128]{1,0:T(8,128)S(1)} %fusion.49), channel_id=1, source_target_pairs={{0,2},{1,3},{2,0},{3,1},{4,6},{5,7},{6,4},{7,5},{8,10},{9,11},{10,... | collective-permute-start | bytes 786440 | tf_op jit(solution)/shard_map/ppermute | solution.py:34
  223.6 12.4 %collective-permute-start.8 = (f32[512,128]{1,0:T(8,128)S(1)}, f32[512,128]{1,0:T(8,128)}, u32[]{:S(2)}, u32[]{:S(2)}) collective-permute-start(f32[512,128]{1,0:T(8,128)S(1)} %fusion.47), channel_id=1, source_target_pairs={{0,3},{1,2},{2,1},{3,0},{4,7},{5,6},{6,5},{7,4},{8,11},{9,10},{10,... | collective-permute-start | bytes 786440 | tf_op jit(solution)/shard_map/ppermute | solution.py:34
  226.1 9.9 %copy-start.7 = (bf16[512,128]{1,0:T(8,128)(2,1)S(1)}, bf16[512,128]{1,0:T(8,128)(2,1)}, u32[]{:S(2)}) copy-start(bf16[512,128]{1,0:T(8,128)(2,1)} %param.11) | copy-start | bytes 393220
  237.4 9.9 %collective-permute-start.10 = (bf16[512,128]{1,0:T(8,128)(2,1)S(1)}, bf16[512,128]{1,0:T(8,128)(2,1)S(1)}, u32[]{:S(2)}, u32[]{:S(2)}) collective-permute-start(bf16[512,128]{1,0:T(8,128)(2,1)S(1)} %get-tuple-element.22), channel_id=1, source_target_pairs={{0,2},{1,3},{2,0},{3,1},{4,6},{5,7},{6,4},{7,5},{8,10},{9,11},{10,... | collective-permute-start | bytes 393224 | tf_op jit(solution)/shard_map/ppermute | solution.py:34
  238.7 8.5 %collective-permute-start.9 = (bf16[512,128]{1,0:T(8,128)(2,1)S(1)}, bf16[512,128]{1,0:T(8,128)(2,1)S(1)}, u32[]{:S(2)}, u32[]{:S(2)}) collective-permute-start(bf16[512,128]{1,0:T(8,128)(2,1)S(1)} %get-tuple-element.22), channel_id=1, source_target_pairs={{0,1},{1,0},{2,3},{3,2},{4,5},{5,4},{6,7},{7,6},{8,9},{9,8},{10,11... | collective-permute-start | bytes 393224 | tf_op jit(solution)/shard_map/ppermute | solution.py:34
  239.5 7.8 %collective-permute-start.11 = (bf16[512,128]{1,0:T(8,128)(2,1)S(1)}, bf16[512,128]{1,0:T(8,128)(2,1)S(1)}, u32[]{:S(2)}, u32[]{:S(2)}) collective-permute-start(bf16[512,128]{1,0:T(8,128)(2,1)S(1)} %get-tuple-element.22), channel_id=1, source_target_pairs={{0,3},{1,2},{2,1},{3,0},{4,7},{5,6},{6,5},{7,4},{8,11},{9,10},{10,... | collective-permute-start | bytes 393224 | tf_op jit(solution)/shard_map/ppermute | solution.py:34
  243.2 21.7 %all-to-all-start.1 = ((bf16[8,3,128,128]{3,2,1,0:T(8,128)(2,1)}), bf16[8,3,128,128]{3,2,1,0:T(8,128)(2,1)S(1)}, u32[]{:S(2)}, u32[]{:S(2)}) async-start(bf16[8,3,128,128]{3,2,1,0:T(8,128)(2,1)} %bitcast.43), calls=%async_computation.1 | async-start | bytes 1572864 | tf_op jit(solution)/shard_map/all_to_all | solution.py:360
  247.4 3.6 %copy-start.1 = (bf16[512,4096]{1,0:T(8,128)(2,1)S(1)}, bf16[512,4096]{1,0:T(8,128)(2,1)}, u32[]{:S(2)}) copy-start(bf16[512,4096]{1,0:T(8,128)(2,1)} %get-tuple-element.15) | copy-start | bytes 12582916
  253.0 11.2 %collective-permute-start.12 = (bf16[576,512]{1,0:T(8,128)(2,1)S(1)}, bf16[576,512]{1,0:T(8,128)(2,1)S(1)}, u32[]{:S(2)}, u32[]{:S(2)}) collective-permute-start(bf16[576,512]{1,0:T(8,128)(2,1)S(1)} %pad_maximum_fusion), channel_id=1, source_target_pairs={{0,16},{16,0},{1,17},{17,1},{2,18},{18,2},{3,19},{19,3},{4,20},{20... | collective-permute-start | bytes 1769480 | tf_op jit(solution)/shard_map/ppermute | solution.py:34
  253.2 9.3 %collective-permute-start.13 = (bf16[576,512]{1,0:T(8,128)(2,1)S(1)}, bf16[576,512]{1,0:T(8,128)(2,1)S(1)}, u32[]{:S(2)}, u32[]{:S(2)}) collective-permute-start(bf16[576,512]{1,0:T(8,128)(2,1)S(1)} %pad_maximum_fusion.1), channel_id=1, source_target_pairs={{0,16},{16,0},{1,17},{17,1},{2,18},{18,2},{3,19},{19,3},{4,20},{20... | collective-permute-start | bytes 1769480 | tf_op jit(solution)/shard_map/ppermute | solution.py:34
  253.7 5.0 %collective-permute-start.15 = (bf16[576,512]{1,0:T(8,128)(2,1)S(1)}, bf16[576,512]{1,0:T(8,128)(2,1)S(1)}, u32[]{:S(2)}, u32[]{:S(2)}) collective-permute-start(bf16[576,512]{1,0:T(8,128)(2,1)S(1)} %pad_maximum_fusion.2), channel_id=1, source_target_pairs={{0,16},{16,0},{1,17},{17,1},{2,18},{18,2},{3,19},{19,3},{4,20},{20... | collective-permute-start | bytes 1769480 | tf_op jit(solution)/shard_map/ppermute | solution.py:34
  254.0 3.6 %collective-permute-start.17 = (bf16[576,512]{1,0:T(8,128)(2,1)S(1)}, bf16[576,512]{1,0:T(8,128)(2,1)S(1)}, u32[]{:S(2)}, u32[]{:S(2)}) collective-permute-start(bf16[576,512]{1,0:T(8,128)(2,1)S(1)} %pad_maximum_fusion.3), channel_id=1, source_target_pairs={{0,16},{16,0},{1,17},{17,1},{2,18},{18,2},{3,19},{19,3},{4,20},{20... | collective-permute-start | bytes 1769480 | tf_op jit(solution)/shard_map/ppermute | solution.py:34
  258.6 34.3 %collective-permute-start.18 = (bf16[576,512]{1,0:T(8,128)(2,1)}, bf16[576,512]{1,0:T(8,128)(2,1)}, u32[]{:S(2)}, u32[]{:S(2)}) collective-permute-start(bf16[576,512]{1,0:T(8,128)(2,1)} %fusion.6), channel_id=1, source_target_pairs={{0,4},{4,0},{8,12},{12,8},{1,5},{5,1},{9,13},{13,9},{2,6},{6,2},{1... | collective-permute-start | bytes 1769480 | tf_op jit(solution)/shard_map/ppermute | solution.py:34
  259.8 43.0 %collective-permute-start.16 = (bf16[576,512]{1,0:T(8,128)(2,1)}, bf16[576,512]{1,0:T(8,128)(2,1)}, u32[]{:S(2)}, u32[]{:S(2)}) collective-permute-start(bf16[576,512]{1,0:T(8,128)(2,1)} %fusion.5), channel_id=1, source_target_pairs={{0,8},{4,12},{8,0},{12,4},{1,9},{5,13},{9,1},{13,5},{2,10},{6,14},... | collective-permute-start | bytes 1769480 | tf_op jit(solution)/shard_map/ppermute | solution.py:34
  263.6 53.9 %collective-permute-start.14 = (bf16[576,512]{1,0:T(8,128)(2,1)}, bf16[576,512]{1,0:T(8,128)(2,1)}, u32[]{:S(2)}, u32[]{:S(2)}) collective-permute-start(bf16[576,512]{1,0:T(8,128)(2,1)} %fusion.4), channel_id=1, source_target_pairs={{0,12},{4,8},{8,4},{12,0},{1,13},{5,9},{9,5},{13,1},{2,14},{6,10},... | collective-permute-start | bytes 1769480 | tf_op jit(solution)/shard_map/ppermute | solution.py:34

commit v4 on v3

--- a/solution.py
+++ b/solution.py
@@ -255,14 +255,16 @@
             jax.ShapeDtypeStruct((owners, *w_out.shape), BF16),
             jax.ShapeDtypeStruct(answers.shape, BF16),
         ),
-        in_specs=[anywhere] * 10,
+        in_specs=[pl.BlockSpec(memory_space=pltpu.VMEM)] * 10,
         out_specs=[anywhere] * 4,
         scratch_shapes=[
             dma((6,)), dma((2, 2)), dma((2,)), dma((2,)),
             dma((2, n_dp, 2)), dma((2, n_dp, 2)), dma((2, n_dp, 2)), dma((2, n_dp, 2)),
             dma((owners,)), dma((owners,)),
         ],
-        compiler_params=pltpu.CompilerParams(collective_id=0, has_side_effects=True),
+        compiler_params=pltpu.CompilerParams(
+            collective_id=0, has_side_effects=True, vmem_limit_bytes=24 * 2**20
+        ),
     )(features, *near, w_in, *early, w_out, answers)
 
 

time: 322 us -> 192 us (0.60)
  Pallas kernels: 196 us -> 66.6 us
  starting transfers between devices: 36.9 us -> 44 us
  waiting for transfers between devices: 36.6 us -> 33 us
  matrix products: 18.7 us -> 15.2 us
    pallas_call x1, Pallas kernels: 168 us -> 38.7 us  [gather_all(): pl.pallas_call(gather_kernel, out_shape=(jax.ShapeDtypeStruct((items, n_m...]
    all_to_all x1, starting transfers between devices: 4.12 us -> 10.6 us  [shards(): incoming = exchange(outgoing)]
    dot_general x1, matrix products: 6.87 us -> 3.36 us  [shards(): preact = jnp.dot(f_full, w_full, preferred_element_type=F32)]
  transfers between devices with their start and end apart: 21 -> 21, of which waited for: 7 -> 6; matrix products, arithmetic and copies ran while one was open for 11% -> 19% of each run, Pallas kernels for 9% -> 15%
where the time goes in v4:
time: 192 us; the launch traced here: 191 us
  Pallas kernels  66.6 us (35%)
  starting transfers between devices  44 us (23%)
  waiting for transfers between devices  33 us (17%)
  local copies, waits for them, and re-layouts  21.1 us (11%)
  matrix products  15.2 us (8%)
  other arithmetic  9.63 us (5%)
    pallas_call x1, Pallas kernels, gather_all(): pl.pallas_call(gather_kernel, out_shape=(jax.ShapeDtypeStruct((items, n_m...  38.7 us
    ppermute x15, waiting for transfers between devices, shift(): return lax.ppermute(value, axis, partner_pairs(lax.axis_size(axis), step))  28.7 us
    pallas_call x1, Pallas kernels, sum_rows(): pl.pallas_call(sums_kernel, grid=(levels, rows_own // tile), in_specs=[pl...  27.9 us
    ppermute x15, starting transfers between devices, shift(): return lax.ppermute(value, axis, partner_pairs(lax.axis_size(axis), step))  15 us
    gather x1, local copies, waits for them, and re-layouts, shards(): jnp.take(book, flat_asked, axis=0, mode='clip')  12 us
    all_to_all x1, starting transfers between devices, shards(): incoming = exchange(outgoing)  10.6 us
    all_to_all x1, starting transfers between devices, shards(): all_codes = exchange(jnp.broadcast_to(codes[None], (owners, levels, items)))  6.02 us
    ppermute x1, starting transfers between devices, shards(): left_2 = lax.ppermute(left_1, 'dp', leftward)  4.38 us
  transfers between devices with their start and end apart: 21, of which 6 were waited for; matrix products, arithmetic and copies ran while one was open for 19% of the time, Pallas kernels for 15%

profile of v4, /device:TPU:8, one launch (start us, length us, event | category | flops | bytes accessed | tf_op | source)
XLA Modules:
  0.0 190.8 jit_solution(11040098403999173418)
XLA Ops:
  0.6 3.5 %collective-permute-start.2 = (bf16[512,512]{1,0:T(8,128)(2,1)}, bf16[512,512]{1,0:T(8,128)(2,1)S(1)}, u32[]{:S(2)}, u32[]{:S(2)}) collective-permute-start(bf16[512,512]{1,0:T(8,128)(2,1)} %w_ref.1), channel_id=1, source_target_pairs={{0,4},{4,8},{8,12},{1,5},{5,9},{9,13},{2,6},{6,10},{10,14},{3,7},{... | collective-permute-start | bytes 1572872 | tf_op jit(solution)/shard_map/ppermute | solution.py:287
  4.1 2.4 %collective-permute-start.3 = (bf16[512,512]{1,0:T(8,128)(2,1)}, bf16[512,512]{1,0:T(8,128)(2,1)}, u32[]{:S(2)}, u32[]{:S(2)}) collective-permute-start(bf16[512,512]{1,0:T(8,128)(2,1)} %w_ref.1), channel_id=1, source_target_pairs={{4,0},{8,4},{12,8},{5,1},{9,5},{13,9},{6,2},{10,6},{14,10},{7,3},{... | collective-permute-start | bytes 1572872 | tf_op jit(solution)/shard_map/ppermute | solution.py:288
  6.5 1.6 collective-permute-start
  8.1 1.5 collective-permute-start.1
  9.6 1.3 broadcast_in_dim.27
  10.9 6.0 %all-to-all-start = ((s32[8,3,512]{2,1,0:T(4,128)}), s32[8,3,512]{2,1,0:T(4,128)S(1)}, u32[]{:S(2)}, u32[]{:S(2)}) async-start(s32[8,3,512]{2,1,0:T(4,128)} %broadcast_in_dim.27), calls=%async_computation | async-start | bytes 131072 | tf_op jit(solution)/shard_map/all_to_all | solution.py:293
  17.0 0.7 add_select_fusion.2
  17.7 3.7 %all-to-all-done = s32[8,3,512]{2,1,0:T(4,128)S(1)} async-done(((s32[8,3,512]{2,1,0:T(4,128)}), s32[8,3,512]{2,1,0:T(4,128)S(1)}, u32[]{:S(2)}, u32[]{:S(2)}) %all-to-all-start) | async-done | bytes 49184 | tf_op jit(solution)/shard_map/all_to_all | solution.py:293
  21.9 0.7 select_reduce_fusion
  22.7 2.2 %collective-permute-start.4 = (bf16[512,512]{1,0:T(8,128)(2,1)S(1)}, bf16[512,512]{1,0:T(8,128)(2,1)}, u32[]{:S(2)}, u32[]{:S(2)}) collective-permute-start(bf16[512,512]{1,0:T(8,128)(2,1)S(1)} %collective-permute-done.2.r1_ref), channel_id=1, source_target_pairs={{0,4},{4,8},{8,12},{1,5},{5,9},{9,13},{2,6},{6,10},{10,14},{3,7},{... | collective-permute-start | bytes 1572872 | tf_op jit(solution)/shard_map/ppermute | solution.py:306
  25.0 4.4 %collective-permute-start.5 = (bf16[512,512]{1,0:T(8,128)(2,1)}, bf16[512,512]{1,0:T(8,128)(2,1)}, u32[]{:S(2)}, u32[]{:S(2)}) collective-permute-start(bf16[512,512]{1,0:T(8,128)(2,1)} %collective-permute-done.3.l1_ref), channel_id=1, source_target_pairs={{4,0},{8,4},{12,8},{5,1},{9,5},{13,9},{6,2},{10,6},{14,10},{7,3},{... | collective-permute-start | bytes 1572872 | tf_op jit(solution)/shard_map/ppermute | solution.py:307
  29.4 1.6 convert_reduce_fusion
  31.1 12.0 %gather_fusion = bf16[3072,128]{1,0:T(8,128)(2,1)S(1)} fusion(bf16[24576,128]{1,0:T(8,128)(2,1)} %bitcast.54, s32[3072]{0:T(1024)S(1)} %broadcast_clamp_fusion), kind=kCustom, calls=%fused_computation | custom fusion | bytes 1585152 | tf_op jit(solution)/shard_map/jit(_take)/gather | solution.py:314
  43.2 1.0 copy-done.5
  44.2 38.7 %shard_map.85 = (bf16[512,4096]{1,0:T(8,128)(2,1)S(1)}, bf16[8,512,512]{2,1,0:T(8,128)(2,1)S(1)}, bf16[8,64,512]{2,1,0:T(8,128)(2,1)S(1)}, bf16[8,3,128,128]{3,2,1,0:T(8,128)(2,1)S(1)}) custom-call(bf16[512,1024]{1,0:T(8,128)(2,1)S(1)} %copy-done.2, bf16[512,1024]{1,0:T(8,128)(2,1)} %collective-permute-done.fx_ref, ...), custom_call_target="tpu_custom_call" | custom-call | tf_op jit(solution)/shard_map/pallas_call | solution.py:250
  83.0 3.4 %multiply_convert_fusion = (bf16[512,512]{1,0:T(8,128)(2,1)S(1)}, f32[512,512]{1,0:T(8,128)}) fusion(bf16[512,4096]{1,0:T(8,128)(2,1)S(1)} %get-tuple-element.15, bf16[4096,512]{1,0:T(8,128)(2,1)S(1)} %bitcast.53), kind=kOutput, calls=%fused_computation.29 | convolution fusion | flops 2148794368 | bytes 9961472 | tf_op jit(solution)/shard_map/dot_general | solution.py:329
  87.3 1.3 collective-permute-start.6
  88.6 1.7 collective-permute-start.7
  90.2 0.6 collective-permute-start.8
  90.8 0.6 multiply_add_fusion
  91.5 0.6 pad_clamp_fusion
  92.1 3.7 %gather_fusion.1 = bf16[1536,128]{1,0:T(8,128)(2,1)S(1)} fusion(bf16[3072,128]{1,0:T(8,128)(2,1)S(1)} %bitcast.44, s32[2048]{0:T(1024)} %pad_clamp_fusion), kind=kCustom, calls=%fused_computation.1 | custom fusion | bytes 792576 | tf_op jit(solution)/shard_map/jit(_take)/gather | solution.py:322
  95.8 3.6 %collective-permute-done.7 = f32[512,128]{1,0:T(8,128)S(1)} collective-permute-done((f32[512,128]{1,0:T(8,128)S(1)}, f32[512,128]{1,0:T(8,128)S(1)}, u32[]{:S(2)}, u32[]{:S(2)}) %collective-permute-start.7) | collective-permute-done | bytes 262176 | tf_op jit(solution)/shard_map/ppermute | solution.py:34
  99.5 1.4 constant_dynamic-update-slice_fusion.3
  100.9 1.8 collective-permute-start.10
  103.1 1.4 collective-permute-start.11
  104.6 1.2 fusion.2
  105.8 0.9 copy.22
  106.7 10.6 %all-to-all-start.1 = ((bf16[8,3,128,128]{3,2,1,0:T(8,128)(2,1)}), bf16[8,3,128,128]{3,2,1,0:T(8,128)(2,1)S(1)}, u32[]{:S(2)}, u32[]{:S(2)}) async-start(bf16[8,3,128,128]{3,2,1,0:T(8,128)(2,1)} %bitcast.43), calls=%async_computation.1 | async-start | bytes 1572864 | tf_op jit(solution)/shard_map/all_to_all | solution.py:362
  117.4 2.0 %fusion.3 = bf16[512,512]{1,0:T(8,128)(2,1)S(1)} fusion(bf16[512,512]{1,0:T(8,128)(2,1)S(1)} %constant_dynamic-update-slice_fusion, bf16[512,512]{1,0:T(8,128)(2,1)S(1)} %bitcast.51, f32[512,512]{1,0:T(8,128)} %get-tuple-element.29), kind=kOutput, calls=%fused_computation.14 | convolution fusion | flops 270794752 | bytes 2621440 | tf_op jit(solution)/shard_map/dot_general | solution.py:369
  121.0 0.5 convolution_convert_fusion
  121.5 0.5 convolution_convert_fusion.1
  121.9 0.5 convolution_convert_fusion.2
  122.4 0.5 convolution_convert_fusion.3
  125.3 0.5 fusion.13
  125.8 0.5 fusion.16
  127.6 1.0 fusion.6
  128.9 1.0 fusion.5
  129.9 2.6 %collective-permute-start.16 = (bf16[576,512]{1,0:T(8,128)(2,1)}, bf16[576,512]{1,0:T(8,128)(2,1)}, u32[]{:S(2)}, u32[]{:S(2)}) collective-permute-start(bf16[576,512]{1,0:T(8,128)(2,1)} %fusion.5), channel_id=1, source_target_pairs={{0,8},{4,12},{8,0},{12,4},{1,9},{5,13},{9,1},{13,5},{2,10},{6,14},... | collective-permute-start | bytes 1769480 | tf_op jit(solution)/shard_map/ppermute | solution.py:34
  132.5 1.0 fusion.4
  133.5 0.6 collective-permute-start.14
  134.3 0.6 all-to-all-done.1
  134.9 27.9 %shard_map.86 = f32[3,8192,128]{2,1,0:T(8,128)} custom-call(s32[3,1,1024]{2,1,0:T(1,128)S(1)} %bitcast.52, bf16[3,1024,128]{2,1,0:T(8,128)(2,1)S(1)} %bitcast.46), custom_call_target="tpu_custom_call" | custom-call | flops 6442450944 | bytes 12582912 | tf_op jit(solution)/shard_map/pallas_call | solution.py:50
  162.9 10.0 %collective-permute-done.16 = bf16[576,512]{1,0:T(8,128)(2,1)} collective-permute-done((bf16[576,512]{1,0:T(8,128)(2,1)}, bf16[576,512]{1,0:T(8,128)(2,1)}, u32[]{:S(2)}, u32[]{:S(2)}) %collective-permute-start.16) | collective-permute-done | bytes 589856 | tf_op jit(solution)/shard_map/ppermute | solution.py:34
  172.8 14.7 %collective-permute-done.14 = bf16[576,512]{1,0:T(8,128)(2,1)} collective-permute-done((bf16[576,512]{1,0:T(8,128)(2,1)}, bf16[576,512]{1,0:T(8,128)(2,1)}, u32[]{:S(2)}, u32[]{:S(2)}) %collective-permute-start.14) | collective-permute-done | bytes 589856 | tf_op jit(solution)/shard_map/ppermute | solution.py:34
  187.5 1.6 convert_add_fusion
  189.1 0.7 slice.31
  189.7 1.0 slice.30
  (85 shorter events, 7.9 us)
Async XLA Ops:
  0.6 22.1 %collective-permute-start.2 = (bf16[512,512]{1,0:T(8,128)(2,1)}, bf16[512,512]{1,0:T(8,128)(2,1)S(1)}, u32[]{:S(2)}, u32[]{:S(2)}) collective-permute-start(bf16[512,512]{1,0:T(8,128)(2,1)} %w_ref.1), channel_id=1, source_target_pairs={{0,4},{4,8},{8,12},{1,5},{5,9},{9,13},{2,6},{6,10},{10,14},{3,7},{... | collective-permute-start | bytes 1572872 | tf_op jit(solution)/shard_map/ppermute | solution.py:287
  4.1 18.6 %collective-permute-start.3 = (bf16[512,512]{1,0:T(8,128)(2,1)}, bf16[512,512]{1,0:T(8,128)(2,1)}, u32[]{:S(2)}, u32[]{:S(2)}) collective-permute-start(bf16[512,512]{1,0:T(8,128)(2,1)} %w_ref.1), channel_id=1, source_target_pairs={{4,0},{8,4},{12,8},{5,1},{9,5},{13,9},{6,2},{10,6},{14,10},{7,3},{... | collective-permute-start | bytes 1572872 | tf_op jit(solution)/shard_map/ppermute | solution.py:288
  6.5 36.6 %collective-permute-start = (bf16[512,1024]{1,0:T(8,128)(2,1)}, bf16[512,1024]{1,0:T(8,128)(2,1)}, u32[]{:S(2)}, u32[]{:S(2)}) collective-permute-start(bf16[512,1024]{1,0:T(8,128)(2,1)} %f_ref.1), channel_id=1, source_target_pairs={{0,1},{1,0},{2,3},{3,2},{4,5},{5,4},{6,7},{7,6},{8,9},{9,8},{10,11... | collective-permute-start | bytes 3145736 | tf_op jit(solution)/shard_map/ppermute | solution.py:34
  8.1 35.1 %collective-permute-start.1 = (bf16[512,1024]{1,0:T(8,128)(2,1)}, bf16[512,1024]{1,0:T(8,128)(2,1)}, u32[]{:S(2)}, u32[]{:S(2)}) collective-permute-start(bf16[512,1024]{1,0:T(8,128)(2,1)} %f_ref.1), channel_id=1, source_target_pairs={{0,2},{1,3},{2,0},{3,1},{4,6},{5,7},{6,4},{7,5},{8,10},{9,11},{10,... | collective-permute-start | bytes 3145736 | tf_op jit(solution)/shard_map/ppermute | solution.py:34
  10.9 10.5 %all-to-all-start = ((s32[8,3,512]{2,1,0:T(4,128)}), s32[8,3,512]{2,1,0:T(4,128)S(1)}, u32[]{:S(2)}, u32[]{:S(2)}) async-start(s32[8,3,512]{2,1,0:T(4,128)} %broadcast_in_dim.27), calls=%async_computation | async-start | bytes 131072 | tf_op jit(solution)/shard_map/all_to_all | solution.py:293
  22.6 2.3 %copy-start.9 = (s32[8,3,128]{2,1,0:T(4,128)}, s32[8,3,128]{2,1,0:T(4,128)S(1)}, u32[]{:S(2)}) copy-start(s32[8,3,128]{2,1,0:T(4,128)S(1)} %select_reduce_fusion) | copy-start | bytes 36868
  22.7 20.4 %copy-start.4 = (bf16[512,512]{1,0:T(8,128)(2,1)}, bf16[512,512]{1,0:T(8,128)(2,1)S(1)}, u32[]{:S(2)}) copy-start(bf16[512,512]{1,0:T(8,128)(2,1)S(1)} %collective-permute-done.2.r1_ref) | copy-start | bytes 1572868
  22.7 20.4 %collective-permute-start.4 = (bf16[512,512]{1,0:T(8,128)(2,1)S(1)}, bf16[512,512]{1,0:T(8,128)(2,1)}, u32[]{:S(2)}, u32[]{:S(2)}) collective-permute-start(bf16[512,512]{1,0:T(8,128)(2,1)S(1)} %collective-permute-done.2.r1_ref), channel_id=1, source_target_pairs={{0,4},{4,8},{8,12},{1,5},{5,9},{9,13},{2,6},{6,10},{10,14},{3,7},{... | collective-permute-start | bytes 1572872 | tf_op jit(solution)/shard_map/ppermute | solution.py:306
  25.0 18.2 %collective-permute-start.5 = (bf16[512,512]{1,0:T(8,128)(2,1)}, bf16[512,512]{1,0:T(8,128)(2,1)}, u32[]{:S(2)}, u32[]{:S(2)}) collective-permute-start(bf16[512,512]{1,0:T(8,128)(2,1)} %collective-permute-done.3.l1_ref), channel_id=1, source_target_pairs={{4,0},{8,4},{12,8},{5,1},{9,5},{13,9},{6,2},{10,6},{14,10},{7,3},{... | collective-permute-start | bytes 1572872 | tf_op jit(solution)/shard_map/ppermute | solution.py:307
  31.1 12.1 %copy-start.2 = (bf16[512,1024]{1,0:T(8,128)(2,1)S(1)}, bf16[512,1024]{1,0:T(8,128)(2,1)}, u32[]{:S(2)}) copy-start(bf16[512,1024]{1,0:T(8,128)(2,1)} %f_ref.1) | copy-start | bytes 3145732
  31.1 12.1 %copy-start.3 = (bf16[512,512]{1,0:T(8,128)(2,1)S(1)}, bf16[512,512]{1,0:T(8,128)(2,1)}, u32[]{:S(2)}) copy-start(bf16[512,512]{1,0:T(8,128)(2,1)} %w_ref.1) | copy-start | bytes 1572868
  31.1 12.1 %copy-start.8 = (bf16[64,512]{1,0:T(8,128)(2,1)S(1)}, bf16[64,512]{1,0:T(8,128)(2,1)}, u32[]{:S(2)}) copy-start(bf16[64,512]{1,0:T(8,128)(2,1)} %o_ref.1) | copy-start | bytes 196612
  43.2 1.0 copy-start.5
  83.0 3.4 %copy-start = (bf16[512,4096]{1,0:T(8,128)(2,1)}, bf16[512,4096]{1,0:T(8,128)(2,1)S(1)}, u32[]{:S(2)}) copy-start(bf16[512,4096]{1,0:T(8,128)(2,1)S(1)} %get-tuple-element.15) | copy-start | bytes 12582916
  83.0 4.0 %copy-start.6 = (bf16[8,64,512]{2,1,0:T(8,128)(2,1)}, bf16[8,64,512]{2,1,0:T(8,128)(2,1)S(1)}, u32[]{:S(2)}) copy-start(bf16[8,64,512]{2,1,0:T(8,128)(2,1)S(1)} %get-tuple-element.17) | copy-start | bytes 1572868
  86.4 4.5 %copy-start.11 = (s32[3,512]{1,0:T(4,128)S(1)}, s32[3,512]{1,0:T(4,128)}, u32[]{:S(2)}) copy-start(s32[3,512]{1,0:T(4,128)} %param.10) | copy-start | bytes 18436
  86.4 4.5 %copy-start.12 = (s32[3,512]{1,0:T(4,128)S(1)}, s32[3,512]{1,0:T(4,128)}, u32[]{:S(2)}) copy-start(s32[3,512]{1,0:T(4,128)} %convert_reduce_fusion) | copy-start | bytes 18436
  86.4 5.7 %copy-start.10 = (s32[8,3,128]{2,1,0:T(4,128)S(1)}, s32[8,3,128]{2,1,0:T(4,128)}, u32[]{:S(2)}) copy-start(s32[8,3,128]{2,1,0:T(4,128)} %copy-done.9) | copy-start | bytes 36868
  87.3 8.5 %collective-permute-start.6 = (f32[512,128]{1,0:T(8,128)S(1)}, f32[512,128]{1,0:T(8,128)S(1)}, u32[]{:S(2)}, u32[]{:S(2)}) collective-permute-start(f32[512,128]{1,0:T(8,128)S(1)} %fusion.51), channel_id=1, source_target_pairs={{0,1},{1,0},{2,3},{3,2},{4,5},{5,4},{6,7},{7,6},{8,9},{9,8},{10,11... | collective-permute-start | bytes 786440 | tf_op jit(solution)/shard_map/ppermute | solution.py:34
  88.6 10.9 %collective-permute-start.7 = (f32[512,128]{1,0:T(8,128)S(1)}, f32[512,128]{1,0:T(8,128)S(1)}, u32[]{:S(2)}, u32[]{:S(2)}) collective-permute-start(f32[512,128]{1,0:T(8,128)S(1)} %fusion.49), channel_id=1, source_target_pairs={{0,2},{1,3},{2,0},{3,1},{4,6},{5,7},{6,4},{7,5},{8,10},{9,11},{10,... | collective-permute-start | bytes 786440 | tf_op jit(solution)/shard_map/ppermute | solution.py:34
  90.2 9.2 %collective-permute-start.8 = (f32[512,128]{1,0:T(8,128)S(1)}, f32[512,128]{1,0:T(8,128)}, u32[]{:S(2)}, u32[]{:S(2)}) collective-permute-start(f32[512,128]{1,0:T(8,128)S(1)} %fusion.47), channel_id=1, source_target_pairs={{0,3},{1,2},{2,1},{3,0},{4,7},{5,6},{6,5},{7,4},{8,11},{9,10},{10,... | collective-permute-start | bytes 786440 | tf_op jit(solution)/shard_map/ppermute | solution.py:34
  92.1 7.5 %copy-start.7 = (bf16[8,64,512]{2,1,0:T(8,128)(2,1)S(1)}, bf16[8,64,512]{2,1,0:T(8,128)(2,1)}, u32[]{:S(2)}) copy-start(bf16[8,64,512]{2,1,0:T(8,128)(2,1)} %copy-done.6) | copy-start | bytes 1572868
  99.5 5.0 %copy-start.13 = (s32[3,512]{1,0:T(4,128)S(1)}, s32[3,512]{1,0:T(4,128)}, u32[]{:S(2)}) copy-start(s32[3,512]{1,0:T(4,128)} %get-tuple-element.26) | copy-start | bytes 18436
  100.9 16.3 %collective-permute-start.10 = (bf16[512,128]{1,0:T(8,128)(2,1)S(1)}, bf16[512,128]{1,0:T(8,128)(2,1)S(1)}, u32[]{:S(2)}, u32[]{:S(2)}) collective-permute-start(bf16[512,128]{1,0:T(8,128)(2,1)S(1)} %get-tuple-element.22), channel_id=1, source_target_pairs={{0,2},{1,3},{2,0},{3,1},{4,6},{5,7},{6,4},{7,5},{8,10},{9,11},{10,... | collective-permute-start | bytes 393224 | tf_op jit(solution)/shard_map/ppermute | solution.py:34
  102.8 14.5 %collective-permute-start.9 = (bf16[512,128]{1,0:T(8,128)(2,1)S(1)}, bf16[512,128]{1,0:T(8,128)(2,1)S(1)}, u32[]{:S(2)}, u32[]{:S(2)}) collective-permute-start(bf16[512,128]{1,0:T(8,128)(2,1)S(1)} %get-tuple-element.22), channel_id=1, source_target_pairs={{0,1},{1,0},{2,3},{3,2},{4,5},{5,4},{6,7},{7,6},{8,9},{9,8},{10,11... | collective-permute-start | bytes 393224 | tf_op jit(solution)/shard_map/ppermute | solution.py:34
  103.1 14.2 %collective-permute-start.11 = (bf16[512,128]{1,0:T(8,128)(2,1)S(1)}, bf16[512,128]{1,0:T(8,128)(2,1)S(1)}, u32[]{:S(2)}, u32[]{:S(2)}) collective-permute-start(bf16[512,128]{1,0:T(8,128)(2,1)S(1)} %get-tuple-element.22), channel_id=1, source_target_pairs={{0,3},{1,2},{2,1},{3,0},{4,7},{5,6},{6,5},{7,4},{8,11},{9,10},{10,... | collective-permute-start | bytes 393224 | tf_op jit(solution)/shard_map/ppermute | solution.py:34
  106.7 28.2 %all-to-all-start.1 = ((bf16[8,3,128,128]{3,2,1,0:T(8,128)(2,1)}), bf16[8,3,128,128]{3,2,1,0:T(8,128)(2,1)S(1)}, u32[]{:S(2)}, u32[]{:S(2)}) async-start(bf16[8,3,128,128]{3,2,1,0:T(8,128)(2,1)} %bitcast.43), calls=%async_computation.1 | async-start | bytes 1572864 | tf_op jit(solution)/shard_map/all_to_all | solution.py:362
  117.4 3.6 %copy-start.1 = (bf16[512,4096]{1,0:T(8,128)(2,1)S(1)}, bf16[512,4096]{1,0:T(8,128)(2,1)}, u32[]{:S(2)}) copy-start(bf16[512,4096]{1,0:T(8,128)(2,1)} %copy-done) | copy-start | bytes 12582916
  123.0 11.1 %collective-permute-start.12 = (bf16[576,512]{1,0:T(8,128)(2,1)S(1)}, bf16[576,512]{1,0:T(8,128)(2,1)S(1)}, u32[]{:S(2)}, u32[]{:S(2)}) collective-permute-start(bf16[576,512]{1,0:T(8,128)(2,1)S(1)} %pad_maximum_fusion), channel_id=1, source_target_pairs={{0,16},{16,0},{1,17},{17,1},{2,18},{18,2},{3,19},{19,3},{4,20},{20... | collective-permute-start | bytes 1769480 | tf_op jit(solution)/shard_map/ppermute | solution.py:34
  123.2 9.3 %collective-permute-start.13 = (bf16[576,512]{1,0:T(8,128)(2,1)S(1)}, bf16[576,512]{1,0:T(8,128)(2,1)S(1)}, u32[]{:S(2)}, u32[]{:S(2)}) collective-permute-start(bf16[576,512]{1,0:T(8,128)(2,1)S(1)} %pad_maximum_fusion.1), channel_id=1, source_target_pairs={{0,16},{16,0},{1,17},{17,1},{2,18},{18,2},{3,19},{19,3},{4,20},{20... | collective-permute-start | bytes 1769480 | tf_op jit(solution)/shard_map/ppermute | solution.py:34
  123.7 5.2 %collective-permute-start.15 = (bf16[576,512]{1,0:T(8,128)(2,1)S(1)}, bf16[576,512]{1,0:T(8,128)(2,1)S(1)}, u32[]{:S(2)}, u32[]{:S(2)}) collective-permute-start(bf16[576,512]{1,0:T(8,128)(2,1)S(1)} %pad_maximum_fusion.2), channel_id=1, source_target_pairs={{0,16},{16,0},{1,17},{17,1},{2,18},{18,2},{3,19},{19,3},{4,20},{20... | collective-permute-start | bytes 1769480 | tf_op jit(solution)/shard_map/ppermute | solution.py:34
  123.9 3.6 %collective-permute-start.17 = (bf16[576,512]{1,0:T(8,128)(2,1)S(1)}, bf16[576,512]{1,0:T(8,128)(2,1)S(1)}, u32[]{:S(2)}, u32[]{:S(2)}) collective-permute-start(bf16[576,512]{1,0:T(8,128)(2,1)S(1)} %pad_maximum_fusion.3), channel_id=1, source_target_pairs={{0,16},{16,0},{1,17},{17,1},{2,18},{18,2},{3,19},{19,3},{4,20},{20... | collective-permute-start | bytes 1769480 | tf_op jit(solution)/shard_map/ppermute | solution.py:34
  128.6 34.3 %collective-permute-start.18 = (bf16[576,512]{1,0:T(8,128)(2,1)}, bf16[576,512]{1,0:T(8,128)(2,1)S(1)}, u32[]{:S(2)}, u32[]{:S(2)}) collective-permute-start(bf16[576,512]{1,0:T(8,128)(2,1)} %fusion.6), channel_id=1, source_target_pairs={{0,4},{4,0},{8,12},{12,8},{1,5},{5,1},{9,13},{13,9},{2,6},{6,2},{1... | collective-permute-start | bytes 1769480 | tf_op jit(solution)/shard_map/ppermute | solution.py:34
  129.9 42.9 %collective-permute-start.16 = (bf16[576,512]{1,0:T(8,128)(2,1)}, bf16[576,512]{1,0:T(8,128)(2,1)}, u32[]{:S(2)}, u32[]{:S(2)}) collective-permute-start(bf16[576,512]{1,0:T(8,128)(2,1)} %fusion.5), channel_id=1, source_target_pairs={{0,8},{4,12},{8,0},{12,4},{1,9},{5,13},{9,1},{13,5},{2,10},{6,14},... | collective-permute-start | bytes 1769480 | tf_op jit(solution)/shard_map/ppermute | solution.py:34
  133.5 54.0 %collective-permute-start.14 = (bf16[576,512]{1,0:T(8,128)(2,1)}, bf16[576,512]{1,0:T(8,128)(2,1)}, u32[]{:S(2)}, u32[]{:S(2)}) collective-permute-start(bf16[576,512]{1,0:T(8,128)(2,1)} %fusion.4), channel_id=1, source_target_pairs={{0,12},{4,8},{8,4},{12,0},{1,13},{5,9},{9,5},{13,1},{2,14},{6,10},... | collective-permute-start | bytes 1769480 | tf_op jit(solution)/shard_map/ppermute | solution.py:34
